TPU v7x, 256 devices: a whole 4x4x8 slice. The times are simulated.
256 devices in a mesh: dp: 4 (over x), head: 2 (over y_hi), ctx: 32 (over z, y_lo, core).
Axes of the slice: x: 4, y: 4 (y_hi: 2, y_lo: 2; y = y_hi * 2 + y_lo), z: 8, core: 2. Of those that a mesh axis runs over, the one named last changes fastest.
Arguments:
- q_latent: bfloat16 [4, 64, 1536], P('dp'), may hold values from -6 to 6
- hidden: bfloat16 [4, 64, 7168], P('dp'), may hold values from -96 to 96
- main_queries: bfloat16 [4, 64, 128, 576], P('dp', 'ctx', 'head'), may hold values from -36 to 36
- main_keys: bfloat16 [4, 32768, 576], P('dp', 'ctx'), may hold values from -6 to 6
- index_keys: bfloat16 [4, 32768, 128], P('dp', 'ctx'), may hold values from -96 to 96
- positions: int32 [4, 64], P('dp'), may hold values from 16384 to 32767, as said below
- w_query: bfloat16 [1536, 8192], P('ctx', 'head'), may hold values from -0.15625 to 0.15625
- w_weights: bfloat16 [7168, 64], P('ctx', 'head'), may hold values from -0.0625 to 0.0625
Outputs:
- grad_query: float32 [1536, 8192], P('ctx', 'head')
- grad_weights: float32 [7168, 64], P('ctx', 'head')
- cross_entropy: float32 [4, 64], P('dp')
Inputs may be any that keep to these rules, and one draw needn't show every extreme that they name: `positions`: in each sequence some query sits at the last key and some at the lowest position.
All inputs are finite; a program needn't handle non-finite values.
Results may differ from a plain program's by a relative error of at most 0.0075.
The roundings to bfloat16 on the way count: a program that leaves them out, or rounds other values in their place, can miss the bound.
Values may be sent and summed in bfloat16 or wider, within the bound.
A program may use at most 128 MiB of HBM per device.

v0:
```python
import jax
import jax.numpy as jnp
from jax import lax
from jax.sharding import PartitionSpec as P

HI = 64
DI = 128
HM = 128
DL = 576


score_scale = 192.0 ** (-0.5)
masked_floor = -1e30


def merged(x, axis, combine):
    everything = jax.tree.map(lambda part: lax.all_gather(part, axis), x)
    initial = jax.tree.map(lambda part: part[0], everything)

    def turn(k, so_far):
        return combine(so_far, jax.tree.map(lambda part: part[k], everything))

    return lax.fori_loop(1, lax.axis_size(axis), turn, initial)


def pair_merge(first, second):
    joined = jnp.maximum(first[0], second[0])
    return (joined, first[1] * jnp.exp(first[0] - joined) + second[1] * jnp.exp(second[0] - joined))


def per_device(
    q_latent, hidden, main_queries, main_keys, index_keys, positions, w_query, w_weights
):
    index_scale = (HI * DI) ** (-0.5)
    ctx_index = lax.axis_index("ctx")
    latent = q_latent[0]
    activations = hidden[0]
    key_main = main_keys[0]
    key_index = index_keys[0]
    query_pos = positions[0]
    ctx_rows = key_main.shape[0]
    rows_latent = w_query.shape[0]
    rows_hidden = w_weights.shape[0]
    heads_here = w_weights.shape[1]
    query_count = latent.shape[0]
    own_latent = lax.dynamic_slice_in_dim(latent, ctx_index * rows_latent, rows_latent, 1)
    own_hidden = lax.dynamic_slice_in_dim(activations, ctx_index * rows_hidden, rows_hidden, 1)
    columns = latent
    query_sum = jnp.dot(
        columns,
        lax.all_gather(w_query, "ctx", axis=0, tiled=True),
        preferred_element_type=jnp.float32,
    )
    columns = activations
    weight_sum = jnp.dot(
        columns,
        lax.all_gather(w_weights, "ctx", axis=0, tiled=True),
        preferred_element_type=jnp.float32,
    )
    index_query = query_sum.astype(jnp.bfloat16).reshape(query_count, heads_here, DI)
    key_positions = ctx_index * ctx_rows + jnp.arange(ctx_rows, dtype=jnp.int32)
    visible = key_positions[None, :] <= query_pos[:, None]
    affinity = jnp.einsum("qjd,sd->qjs", index_query, key_index, preferred_element_type=jnp.float32)
    partial_logits = (
        jnp.sum(weight_sum[:, :, None] * jnp.maximum(affinity, 0.0), axis=1) * index_scale
    )
    logits = lax.psum(partial_logits, "head")
    gathered = lax.all_gather(main_queries[0], "ctx", axis=0, tiled=True)
    block_count = gathered.shape[1] // 8
    blocks = gathered.reshape(query_count, block_count, 8, DL).transpose(1, 0, 2, 3)

    def block_scores(block):
        scores = (
            jnp.einsum("qhd,sd->qhs", block, key_main, preferred_element_type=jnp.float32)
            * score_scale
        )
        return jnp.where(visible[:, None, :], scores, masked_floor)

    def local_moments(block):
        scores = block_scores(block)
        local_max = jnp.max(scores, axis=2)
        shifted = jnp.where(visible[:, None, :], jnp.exp(scores - local_max[:, :, None]), 0.0)
        return (local_max, jnp.sum(shifted, axis=2))

    local_max, local_sum = lax.map(local_moments, blocks)
    index_local = jnp.max(jnp.where(visible, logits, masked_floor), axis=1)
    index_total = jnp.sum(jnp.where(visible, jnp.exp(logits - index_local[:, None]), 0.0), axis=1)
    main_max, main_sum = merged((local_max, local_sum), "ctx", pair_merge)
    index_max, index_sum = merged((index_local, index_total), "ctx", pair_merge)

    def add_probs(running, inputs):
        block, block_max, block_sum = inputs
        scores = block_scores(block)
        shifted = jnp.where(visible[:, None, :], jnp.exp(scores - block_max[:, :, None]), 0.0)
        return (running + jnp.sum(shifted / block_sum[:, :, None], axis=1), None)

    target_part, _ = lax.scan(
        add_probs, jnp.zeros((query_count, ctx_rows), jnp.float32), (blocks, main_max, main_sum)
    )
    target = lax.psum(target_part, "head") / HM
    shifted = jnp.where(visible, jnp.exp(logits - index_max[:, None]), 0.0)
    index_probs = shifted / index_sum[:, None]
    log_probs = logits - (index_max + jnp.log(index_sum))[:, None]
    loss_part = -jnp.sum(jnp.where(visible, target * log_probs, 0.0), axis=1)
    delta = jnp.where(visible, index_probs - target, 0.0)
    score_grad = jnp.where(
        affinity > 0, delta[:, None, :] * weight_sum[:, :, None] * index_scale, 0.0
    ).astype(jnp.bfloat16)
    query_grad = jnp.einsum(
        "qjs,sd->qjd", score_grad, key_index, preferred_element_type=jnp.float32
    )
    weight_grad = jnp.sum(delta[:, None, :] * jnp.maximum(affinity, 0.0), axis=2) * index_scale
    query_grad, weight_grad, cross_entropy = lax.psum((query_grad, weight_grad, loss_part), "ctx")
    query_bf = query_grad.reshape(query_count, heads_here * DI).astype(jnp.bfloat16)
    weight_bf = weight_grad.astype(jnp.bfloat16)
    grad_query = jnp.einsum("qr,qc->rc", own_latent, query_bf, preferred_element_type=jnp.float32)
    grad_weights = jnp.einsum(
        "qr,qc->rc", own_hidden, weight_bf, preferred_element_type=jnp.float32
    )
    grad_query, grad_weights = lax.psum((grad_query, grad_weights), "dp")
    return (grad_query, grad_weights, cross_entropy[None, :])


def solution(mesh):
    return jax.shard_map(
        per_device,
        mesh=mesh,
        in_specs=(
            P("dp", None, None),
            P("dp", None, None),
            P("dp", "ctx", "head", None),
            P("dp", "ctx", None),
            P("dp", "ctx", None),
            P("dp", None),
            P("ctx", "head"),
            P("ctx", "head"),
        ),
        out_specs=(P("ctx", "head"), P("ctx", "head"), P("dp", None)),
        check_vma=False,
    )
```

profile of v0, /device:TPU:1, one launch (start us, length us, event | category | flops | bytes accessed | tf_op | source)
XLA Modules:
  0.0 571.2 jit_solution(4677835207720997851)
XLA Ops:
  8.7 40.4 %all-gather.5 = bf16[32,224,32]{1,2,0:T(8,128)(2,1)S(1)} all-gather(bf16[1,224,32]{1,2,0:T(8,128)(2,1)} %bitcast.120), channel_id=1, replica_groups=mesh['dp'=4,'head'=2,'ctx'=32] {'ctx'}, dimensions={0}, use_global_device_ids=true | all-gather | bytes 473088 | tf_op jit(solution)/shard_map/all_gather | solution.py:57
  50.7 32.6 %all-gather.11.cloned.1.call-done = bf16[1,64,64,576]{3,2,0,1:T(8,128)(2,1)} async-done(((bf16[1,2,64,576]{3,2,0,1:T(8,128)(2,1)}), bf16[1,64,64,576]{3,2,0,1:T(8,128)(2,1)}) %all-gather.11.cloned.1.call-update) | async-done | bytes 4718608 | tf_op jit(solution)/shard_map/all_gather | solution.py:68
  83.2 5.3 copy.32
  88.5 30.0 %while.60 = (s32[]{:T(128)}, f32[8,64,8]{1,2,0:T(8,128)S(1)}, f32[8,64,8]{1,2,0:T(8,128)S(1)}, bf16[8,64,8,576]{3,2,1,0:T(8,128)(2,1)}, bf16[1024,576]{0,1:T(8,1...) while((s32[]{:T(128)}, f32[8,64,8]{1,2,0:T(8,128)S(1)}, f32[8,64,8]{1,2,0:T(8,128)S(1)}, ...), condition=%wide.region_9.10_spmd.clone, body=%wide.region_6.9_spmd.clone.sunk | while | flops 608238592 | bytes 6261593 | solution.py:85
  88.6 2.7 fusion.57
  92.4 2.7 fusion.57
  96.1 2.7 fusion.57
  99.9 2.7 fusion.57
  103.6 2.7 fusion.57
  107.4 2.7 fusion.57
  111.2 2.7 fusion.57
  115.0 2.7 fusion.57
  118.6 37.2 %all-gather.3 = f32[256,64,8]{1,2,0:T(8,128)S(1)} all-gather(f32[8,64,8]{1,2,0:T(8,128)S(1)} %get-tuple-element.341), channel_id=5, replica_groups=mesh['dp'=4,'head'=2,'ctx'=32] {'ctx'}, dimensions={0}, use_global_device_ids=true | all-gather | bytes 540672 | tf_op jit(solution)/shard_map/all_gather | solution.py:17
  155.8 36.0 %all-gather.4 = f32[256,64,8]{1,2,0:T(8,128)S(1)} all-gather(f32[8,64,8]{1,2,0:T(8,128)S(1)} %get-tuple-element.342), channel_id=6, replica_groups=mesh['dp'=4,'head'=2,'ctx'=32] {'ctx'}, dimensions={0}, use_global_device_ids=true | all-gather | bytes 540672 | tf_op jit(solution)/shard_map/all_gather | solution.py:17
  193.6 30.3 %while.61 = (s32[]{:T(128)}, f32[64,1024]{1,0:T(8,128)S(1)}, bf16[8,64,8,576]{3,2,1,0:T(8,128)(2,1)}, bf16[1024,576]{0,1:T(8,128)(2,1)}, f32[8,64,8]{1,2,0:T(8,1...) while((s32[]{:T(128)}, f32[64,1024]{1,0:T(8,128)S(1)}, ...), condition=%wide.region_14.15_spmd.clone, body=%wide.region_12.14_spmd.clone.sunk | while | flops 607256576 | bytes 3040115 | solution.py:97
  193.9 3.4 fusion.60
  197.7 3.4 fusion.60
  201.5 3.4 fusion.60
  205.3 3.4 fusion.60
  209.1 3.4 fusion.60
  212.8 3.4 fusion.60
  216.6 3.4 fusion.60
  220.4 3.4 fusion.60
  224.0 7.0 %fusion.20 = bf16[8,8,32,128]{3,1,2,0:T(8,128)(2,1)S(1)} fusion(bf16[1536,4096]{1,0:T(8,128)(2,1)} %all-gather.9.cloned.1.call-done, bf16[1,64,1536]{2,1,0:T(8,128)(2,1)S(1)} %copy-done.3), kind=kOutput, calls=%fused_computation.39 | convolution fusion | flops 805568512 | bytes 13303808 | tf_op jit(solution)/shard_map/dot_general | solution.py:49
  231.1 4.0 multiply_reduce_fusion.1
  237.2 41.2 %all-reduce.11.cloned.1.call-done = (f32[64,1024]{1,0:T(8,128)}, f32[64,1024]{1,0:T(8,128)}) async-done(((f32[64,1024]{1,0:T(8,128)}, f32[64,1024]{1,0:T(8,128)}), (f32[64,1024]{1,0:T(8,128)}, f32[64,1024]{1,0:T(8,128)})) %all-reduce.11.cloned.1.call-update) | async-done | bytes 524304 | tf_op jit(solution)/shard_map/psum | solution.py:67
  281.3 103.5 %all-reduce.3 = (f32[2048]{0:T(1024)S(1)}, f32[2048]{0:T(1024)S(1)}) all-reduce(f32[2048]{0:T(1024)S(1)} %dynamic-update-slice, f32[2048]{0:T(1024)S(1)} %dynamic-update-slice.1), channel_id=2, replica_groups=mesh['dp'=4,'head'=2,'ctx'=32] {'ctx'}, use_global_device_ids=true, to_apply=%add | all-reduce | flops 4096 | bytes 32768
  387.7 4.4 multiply_reduce_fusion
  395.0 116.9 %all-reduce.12 = (bf16[64,32,128]{2,1,0:T(8,128)(2,1)S(1)}, bf16[64,32]{1,0:T(8,128)(2,1)S(1)}, f32[1,64]{1,0:T(1,128)}) all-reduce(f32[64,32,128]{2,1,0:T(8,128)S(1)} %fusion.19, f32[64,32]{1,0:T(8,128)S(1)} %broadcast_multiply_fusion.1, f32[1,64]{1,0:T(1,128)S(1)} %negate_bitcast_fusion), channel_id=1, replica_groups=mesh['dp'=4,'head'=2,'ctx'=32] {'ctx'}, use_global_device_ids=true, to_apply=%region_16.17 | all-reduce | flops 264256 | bytes 1585664 | tf_op jit(solution)/shard_map/psum | solution.py:113
  513.5 13.8 %psum.54 = f32[224,32]{0,1:T(8,128)} all-reduce(f32[224,32]{0,1:T(8,128)S(1)} %fusion.35), channel_id=1, replica_groups=mesh['dp'=4,'head'=2,'ctx'=32] {'dp'}, use_global_device_ids=true, to_apply=%region_20.21 | all-reduce | flops 7168 | bytes 57344 | tf_op jit(solution)/shard_map/psum | solution.py:120
  527.3 35.3 %all-reduce.9.cloned.1.call-done = f32[48,4096]{1,0:T(8,128)} async-done(((f32[48,4096]{1,0:T(8,128)}), f32[48,4096]{1,0:T(8,128)}) %all-reduce.9.cloned.1.call-update) | async-done | bytes 786448 | tf_op jit(solution)/shard_map/psum | solution.py:120
  562.6 2.1 copy.105
  (196 shorter events, 29.5 us)
Async XLA Ops:
  7.2 43.1 %copy-start = (bf16[1,64,7168]{2,1,0:T(8,128)(2,1)S(1)}, bf16[1,64,7168]{2,1,0:T(8,128)(2,1)}, u32[]{:S(2)}) copy-start(bf16[1,64,7168]{2,1,0:T(8,128)(2,1)} %param.17) | copy-start | bytes 2752516
  7.2 76.1 %all-gather.11.cloned.1.call-start = ((), (), s32[]{:S(2)}) async-start(), calls=%async_computation.2 | async-start | bytes 5406720 | tf_op jit(solution)/shard_map/all_gather | solution.py:68
  7.9 216.0 %all-gather.9.cloned.1.call-start = ((), (), s32[]{:S(2)}) async-start(), calls=%async_computation | async-start | bytes 12976128 | tf_op jit(solution)/shard_map/all_gather | solution.py:51
  8.7 269.7 %all-reduce.11.cloned.1.call-start = ((), (), s32[]{:S(2)}) async-start(), calls=%async_computation.3 | async-start | bytes 1048576 | tf_op jit(solution)/shard_map/psum | solution.py:67
  83.2 5.3 copy-start.5
  193.6 30.4 %copy-start.3 = (bf16[1,64,1536]{2,1,0:T(8,128)(2,1)S(1)}, bf16[1,64,1536]{2,1,0:T(8,128)(2,1)}, u32[]{:S(2)}) copy-start(bf16[1,64,1536]{2,1,0:T(8,128)(2,1)} %param.16) | copy-start | bytes 589828
  223.9 7.1 %copy-start.2 = (f32[64,1024]{1,0:T(8,128)}, f32[64,1024]{1,0:T(8,128)S(1)}, u32[]{:S(2)}) copy-start(f32[64,1024]{1,0:T(8,128)S(1)} %get-tuple-element.345) | copy-start | bytes 786436
  223.9 7.2 %copy-start.4 = (bf16[1,1024,128]{2,1,0:T(8,128)(2,1)S(1)}, bf16[1,1024,128]{2,1,0:T(8,128)(2,1)}, u32[]{:S(2)}) copy-start(bf16[1,1024,128]{2,1,0:T(8,128)(2,1)} %param.20) | copy-start | bytes 786436
  231.1 4.8 copy-start.6
  235.9 326.7 %all-reduce.9.cloned.1.call-start = ((), (), s32[]{:S(2)}) async-start(), calls=%async_computation.1 | async-start | bytes 1572864 | tf_op jit(solution)/shard_map/psum | solution.py:120
  387.7 5.8 %copy-start.1 = (f32[64,32,1024]{2,1,0:T(8,128)S(1)}, f32[64,32,1024]{2,1,0:T(8,128)}, u32[]{:S(2)}) copy-start(f32[64,32,1024]{2,1,0:T(8,128)} %get-tuple-element.520) | copy-start | bytes 25165828
Sparse Core Ops, SparseCore 0:
  9.9 73.3 all-gather.10
  85.1 97.1 all-gather.8
  236.0 42.3 all-reduce.10
  513.4 49.1 all-reduce.8
where the time goes:
time: 573 us; the launch traced here: 571 us
  blocking collectives  348 us (61%)
  waiting for transfers between devices  110 us (19%)
  matrix products  63.1 us (11%)
  other arithmetic  19.4 us (3%)
  between operations  14.7 us (3%)
  local copies, waits for them, and re-layouts  13.7 us (2%)
    psum x1, blocking collectives, per_device(): lax.psum((query_grad, weight_grad, loss_part), 'ctx')  117 us
    unnamed x1, blocking collectives  103 us
    all_gather x2, blocking collectives, merged(): everything = jax.tree.map(lambda part: lax.all_gather(part, axis), x)  73.2 us
    dot_general x16, matrix products, block_scores(): jnp.einsum('qhd,sd->qhs', block, key_main, preferred_element_type=jnp.flo...  48.7 us
    psum x1, waiting for transfers between devices, per_device(): logits = lax.psum(partial_logits, 'head')  41.2 us
    all_gather x1, blocking collectives, per_device(): lax.all_gather(w_weights, 'ctx', axis=0, tiled=True)  40.4 us
    psum x1, waiting for transfers between devices, per_device(): grad_query, grad_weights = lax.psum((grad_query, grad_weights), 'dp')  35.3 us
    all_gather x1, waiting for transfers between devices, per_device(): gathered = lax.all_gather(main_queries[0], 'ctx', axis=0, tiled=True)  32.6 us
  transfers between devices with their start and end apart: 4, of which 3 were waited for; matrix products, arithmetic and copies ran while one was open for 12% of the time, Pallas kernels for 0%

commit v1 on v0

v1 whole, which is shorter than its diff:
```python
import jax
import jax.numpy as jnp
from jax import lax
from jax.experimental import pallas as pl
from jax.experimental.pallas import tpu as pltpu
from jax.sharding import PartitionSpec as P

HI = 64
DI = 128
HM = 128
DL = 576
MESH = pl.DeviceIdType.MESH
BF = jnp.bfloat16
F32 = jnp.float32

LOG2E = 1.4426950408889634
LN2 = 0.6931471805599453
C2 = 192.0 ** (-0.5) * LOG2E
ISCALE = (HI * DI) ** (-0.5)
FLOOR = -1e30
LOW = -1e29

NT = (((1,), (1,)), ((), ()))
NN = (((1,), (0,)), ((), ()))


def dot(a, b, dims=NN):
    return lax.dot_general(a, b, dims, preferred_element_type=F32)


def log2(x):
    return jnp.log(x) * LOG2E


def remote(src, dst, ss, rs, dev):
    return pltpu.make_async_remote_copy(
        src_ref=src, dst_ref=dst, send_sem=ss, recv_sem=rs, device_id=dev, device_id_type=MESH
    )


def loop(lo, hi, body):
    def turn(i, carry):
        body(i)
        return carry

    lax.fori_loop(lo, hi, turn, 0)


def kernel(
    pos_s, pos_v, lat8, lat_t, hid, hid_t, mq, mk, ik, wq, ww,
    out_q, out_w, out_l,
    WB, IQL, IQY, IQG, HWL, HWY, HWS, HWG, HB, MQ, K2, IK2, E, MA, LA, MB, LB,
    ST, STG, AFF, LM, T, SG, RSB, RSR, WGP, WGR, DISP, QGA, WGS, WGA, LTX, HTX, OUTP,
    s_w, r_w, s_wx, r_wx, s_iqy, r_iqy, s_iqg, r_iqg, s_hwy, r_hwy, s_hwg, r_hwg,
    s_mp, r_mp, s_ra, r_ra, s_la, r_la, s_rb, r_rb, s_lb, r_lb, s_ca, r_ca, s_cb, r_cb,
    s_k, r_k, s_st, r_st, s_rs, r_rs, s_wg, r_wg, s_dq, r_dq, s_dw, r_dw,
    s_lx, r_lx, s_hx, r_hx, s_o, r_o, s_ox, r_ox,
):
    b = lax.axis_index("dp")
    yh = lax.axis_index("head")
    c = lax.axis_index("ctx")
    z = c // 4
    yl = (c // 2) % 2
    core = c % 2
    y = yh * 2 + yl
    u = yl * 2 + core
    g = z * 2 + core
    by = b * 4 + y

    def g_dev(gg):
        return {"dp": b, "head": yh, "ctx": (gg // 2) * 4 + yl * 2 + gg % 2}

    def y_dev(yy):
        return {"dp": b, "head": yy // 2, "ctx": z * 4 + (yy % 2) * 2 + core}

    def x_dev(bb):
        return {"dp": bb, "head": yh, "ctx": c}

    def by_dev(n):
        yy = n % 4
        return {"dp": n // 4, "head": yy // 2, "ctx": z * 4 + (yy % 2) * 2 + core}

    def a_dev(zz, uu):
        return {"dp": b, "head": yh, "ctx": zz * 4 + uu}

    def zm(v):
        return lax.rem(v + 16, 8)

    bar = pltpu.get_barrier_semaphore()

    def hello(dev):
        pl.semaphore_signal(bar, inc=1, device_id=dev, device_id_type=MESH)

    loop(1, 16, lambda d: hello(g_dev(lax.rem(g + d, 16))))
    loop(1, 16, lambda d: hello(by_dev(lax.rem(by + d, 16))))

    def not_self(t, uu):
        return jnp.logical_or(b > 0, jnp.logical_or(t > 0, uu != u))

    def hello_a(i):
        t, uu = i // 4, i % 4

        @pl.when(not_self(t, uu))
        def _():
            hello(a_dev(zm(z - b - 4 * t), uu))
            hello(a_dev(zm(z + b + 4 * t), uu))

    loop(0, 8, hello_a)
    pl.semaphore_wait(bar, jnp.where(b == 0, 44, 46))

    def w_copy(t, uu, slot):
        zd = zm(z - b - 4 * t)
        cols = pl.ds(pl.multiple_of((zd * 4 + uu) * 128, 128), 128)
        return remote(
            wq.at[:, cols], WB.at[b, t, u], s_w.at[t * 4 + uu], r_w.at[t * 4 + slot], a_dev(zd, uu)
        )

    def wx_copy(bb, slot):
        return remote(WB.at[b], WB.at[slot], s_wx.at[bb], r_wx.at[slot], x_dev(bb))

    def iqy_copy(yy, slot):
        return remote(IQL.at[yy], IQY.at[slot], s_iqy.at[yy], r_iqy.at[slot], y_dev(yy))

    def iqg_copy(gg, slot):
        return remote(IQY, IQG.at[slot], s_iqg.at[gg], r_iqg.at[slot], g_dev(gg))

    def hwy_copy(yy, slot):
        return remote(HWL.at[yy], HWY.at[slot], s_hwy.at[yy], r_hwy.at[slot], y_dev(yy))

    def hwg_copy(gg, slot):
        return remote(HWS, HWG.at[slot], s_hwg.at[gg], r_hwg.at[slot], g_dev(gg))

    def st_copy(gg, slot):
        return remote(ST, STG.at[slot], s_st.at[gg], r_st.at[slot], g_dev(gg))

    def rs_copy(gg, slot):
        return remote(RSB.at[gg], RSR.at[slot], s_rs.at[gg], r_rs.at[slot], g_dev(gg))

    def wg_copy(gg, slot):
        return remote(WGP, WGR.at[slot], s_wg.at[gg], r_wg.at[slot], g_dev(gg))

    def dq_copy(n, slot):
        return remote(DISP.at[n % 4], QGA.at[slot], s_dq.at[n], r_dq.at[slot], by_dev(n))

    def dw_copy(n, slot):
        return remote(WGS, WGA.at[slot], s_dw.at[n], r_dw.at[slot], by_dev(n))

    def lx_copy(bb, t, slot):
        return remote(
            lat_t.at[zm(z - bb - 4 * t)], LTX.at[slot, t],
            s_lx.at[bb * 2 + t], r_lx.at[slot * 2 + t], x_dev(bb),
        )

    def hx_copy(bb, slot):
        return remote(hid_t, HTX.at[slot], s_hx.at[bb], r_hx.at[slot], x_dev(bb))

    def o_copy(t, uu, slot):
        zd = zm(z - b - 4 * t)
        cols = pl.ds(pl.multiple_of(c * 128, 128), 128)
        return remote(
            OUTP.at[t, uu], out_q.at[:, cols], s_o.at[t * 4 + uu], r_o.at[t * 4 + slot],
            a_dev(zd, uu),
        )

    def ox_copy(bb, t, slot):
        cols = pl.ds(pl.multiple_of(zm(z + b + 4 * t) * 512, 512), 512)
        return remote(
            out_q.at[:, cols], out_q.at[:, cols],
            s_ox.at[bb * 2 + t], r_ox.at[slot * 2 + t], x_dev(bb),
        )

    def others(n, me, start):
        loop(1, n, lambda d: start(lax.rem(me + d, n)))

    right = {"dp": b, "head": yh, "ctx": zm(z + 1) * 4 + u}
    left = {"dp": b, "head": yh, "ctx": zm(z - 1) * 4 + u}
    twin = {"dp": b, "head": yh, "ctx": z * 4 + yl * 2 + (1 - core)}

    def piece(zz, half):
        return MQ.at[zz * 2 + core, half]

    def ring(kind, k):
        half = yh if kind[1] == "a" else 1 - yh
        zz = zm(z - k) if kind[0] == "r" else zm(z + k)
        ss, rs = {"ra": (s_ra, r_ra), "la": (s_la, r_la), "rb": (s_rb, r_rb), "lb": (s_lb, r_lb)}[kind]
        return remote(
            piece(zz, half), piece(zz, half), ss.at[k], rs.at[k], right if kind[0] == "r" else left
        )

    def to_twin(zz, which):
        half = yh if which == "a" else 1 - yh
        ss, rs = (s_ca, r_ca) if which == "a" else (s_cb, r_cb)
        return remote(piece(zz, half), piece(zz, half), ss.at[zz], rs.at[zz], twin)

    partner = {"dp": b, "head": 1 - yh, "ctx": c}
    mp_copy = remote(mq.at[1 - yh], MQ.at[g, yh], s_mp.at[0], r_mp.at[0], partner)
    up = y_dev(lax.rem(y + 1, 4))
    down = y_dev(lax.rem(y + 3, 4))
    ik_copies = [
        remote(ik.at[0:512], IK2.at[0:512], s_k.at[0], r_k.at[0], up),
        remote(ik.at[512:1024], IK2.at[512:1024], s_k.at[1], r_k.at[1], down),
    ]
    mk_copies = [
        remote(mk.at[0:512], K2.at[0:512], s_k.at[2], r_k.at[2], up),
        remote(mk.at[512:1024], K2.at[512:1024], s_k.at[3], r_k.at[3], down),
    ]

    mp_copy.start()

    def w_start(i):
        t, uu = i // 4, i % 4

        @pl.when(not_self(t, uu))
        def _():
            w_copy(t, uu, u).start()

    loop(0, 8, w_start)
    MQ[g, yh] = mq[yh]
    ring("ra", 0).start()
    ring("la", 0).start()
    to_twin(z, "a").start()
    HWL[...] = dot(hid[...], ww[...]).reshape(4, 16, 128)
    others(4, y, lambda yy: hwy_copy(yy, y).start())
    HWY[y] = HWL[y]
    for one in ik_copies:
        one.start()
    for one in mk_copies:
        one.start()

    @pl.when(b == 0)
    def _():
        WB[0, 0, u] = wq[:, pl.ds(pl.multiple_of(c * 128, 128), 128)]

    for ref in (MA, LA, MB, LB):
        ref[...] = jnp.zeros_like(ref)

    def w_wait(i):
        t, uu = i // 4, i % 4

        @pl.when(not_self(t, uu))
        def _():
            w_copy(t, uu, uu).wait_recv()

    loop(0, 8, w_wait)
    others(4, b, lambda bb: wx_copy(bb, b).start())

    mp_copy.wait_recv()
    ring("rb", 0).start()
    ring("lb", 0).start()
    to_twin(z, "b").start()

    lane = lax.broadcasted_iota(jnp.int32, (128, 128), 1)
    key_row = lax.broadcasted_iota(jnp.int32, (1, 1024), 1)
    c_far = z * 4 + (1 - yl) * 2 + core

    def scores(zz, keys, base, part, m_acc, l_acc):
        q = MQ[pl.ds(zz * 2, 2)].reshape(256, DL)
        s = dot(q, keys[...], NT)
        for i in range(2):
            slot = zz * 2 + i
            vis = key_row + base <= pos_s[slot]
            si = jnp.where(vis, s[i * 128:(i + 1) * 128], FLOOR)
            m = jnp.maximum(jnp.max(si, axis=1, keepdims=True), LOW)
            e = jnp.exp2((si - m) * C2)
            E[part, slot] = e
            here = lane == slot
            m_acc[...] = jnp.where(here, m, m_acc[...])
            l_acc[...] = jnp.where(here, jnp.sum(e, axis=1, keepdims=True), l_acc[...])

    def near(zz):
        to_twin(zz, "a").wait_recv()
        to_twin(zz, "b").wait_recv()
        scores(zz, mk, c * 1024, 0, MA, LA)

    def step(k):
        if k < 4:
            ring("ra", k).wait_recv()
            if k < 3:
                ring("ra", k + 1).start()
            to_twin(zm(z - 1 - k), "a").start()
        if k < 3:
            ring("la", k).wait_recv()
            if k < 2:
                ring("la", k + 1).start()
            to_twin(zm(z + 1 + k), "a").start()
            ring("rb", k).wait_recv()
            if k < 2:
                ring("rb", k + 1).start()
            to_twin(zm(z - 1 - k), "b").start()
        ring("lb", k).wait_recv()
        if k < 3:
            ring("lb", k + 1).start()
        to_twin(zm(z + 1 + k), "b").start()

    step(0)
    near(z)
    others(4, b, lambda bb: wx_copy(bb, bb).wait_recv())
    iq = jnp.zeros((64, 128), F32)
    for bb in range(4):
        for t in range(2):
            iq = iq + dot(lat8[zm(z + bb + 4 * t)], WB[bb, t].reshape(192, 128))
    IQL[...] = iq.astype(BF).reshape(4, 16, 128)
    others(4, y, lambda yy: iqy_copy(yy, y).start())
    IQY[y] = IQL[y]
    others(4, y, lambda yy: hwy_copy(yy, yy).wait_recv())
    HWS[...] = HWY[0] + HWY[1] + HWY[2] + HWY[3]
    others(16, g, lambda gg: hwg_copy(gg, g).start())
    HWG[g] = HWS[...]
    step(1)
    others(4, y, lambda yy: iqy_copy(yy, yy).wait_recv())
    others(16, g, lambda gg: iqg_copy(gg, g).start())
    IQG[g] = IQY[...]
    loop(0, 2, lambda i: near(zm(z - 1 + 2 * i)))
    step(2)
    loop(0, 2, lambda i: near(zm(z - 2 + 4 * i)))
    step(3)
    others(4, b, lambda bb: [lx_copy(bb, t, b).start() for t in range(2)])
    others(4, b, lambda bb: hx_copy(bb, b).start())
    for t in range(2):
        LTX[b, t] = lat_t[zm(z - b - 4 * t)]
    HTX[b] = hid_t[...]
    loop(0, 2, lambda i: near(zm(z - 3 + 6 * i)))
    near(zm(z + 4))

    others(16, g, lambda gg: hwg_copy(gg, gg).wait_recv())
    hw = HWG[0]
    for gg in range(1, 16):
        hw = hw + HWG[gg]
    for gg in range(16):
        for ys in range(4):
            j = (ys // 2) * 32 + (gg // 2) * 4 + (ys % 2) * 2 + gg % 2
            HB[gg * 4 + ys] = jnp.broadcast_to(hw[:, j:j + 1] * ISCALE, (16, 128))
    others(16, g, lambda gg: iqg_copy(gg, gg).wait_recv())
    for one in ik_copies:
        one.wait_recv()
    lane256 = lax.broadcasted_iota(jnp.int32, (16, 256), 1)
    posq = pos_v[...]
    posq = jnp.concatenate([posq, posq], axis=1)

    def index_tile(keys, i, tile, base):
        kt = keys[pl.ds(pl.multiple_of(i * 256, 256), 256), :]
        aff = dot(IQG[...].reshape(1024, 128), kt, NT)
        AFF[tile] = aff
        total = jnp.zeros((16, 256), F32)
        for p in range(64):
            hb = HB[p]
            total = total + jnp.maximum(aff[p * 16:(p + 1) * 16], 0.0) * jnp.concatenate([hb, hb], axis=1)
        vis = lane256 + (base + i * 256) <= posq
        LM[tile] = jnp.where(vis, total * LOG2E, FLOOR)

    loop(0, 4, lambda i: index_tile(ik, i, i, c * 1024))
    loop(0, 4, lambda i: index_tile(IK2, i, i + 4, c_far * 1024))
    lm = LM[...]
    im = jnp.maximum(jnp.max(jnp.max(lm, axis=0), axis=1, keepdims=True), LOW)
    il = jnp.sum(jnp.sum(jnp.exp2(lm - im[None]), axis=0), axis=1, keepdims=True)
    ST[16:32] = jnp.broadcast_to(im + log2(jnp.maximum(il, 1e-37)), (16, 128))

    for one in mk_copies:
        one.wait_recv()
    loop(0, 8, lambda zz: scores(zz, K2, c_far * 1024, 1, MB, LB))
    ma, mb = MA[...], MB[...]
    mx = jnp.maximum(ma, mb)
    ls = LA[...] * jnp.exp2((ma - mx) * C2) + LB[...] * jnp.exp2((mb - mx) * C2)
    ST[0:16] = (mx * C2 + log2(jnp.maximum(ls, 1e-37))).T[0:16]
    others(16, g, lambda gg: st_copy(gg, g).start())
    STG[g] = ST[...]
    others(16, g, lambda gg: st_copy(gg, gg).wait_recv())
    stats = STG[...]
    top = jnp.max(stats, axis=0)
    lse = top + log2(jnp.sum(jnp.exp2(stats - top[None]), axis=0))
    lse_t = jnp.concatenate([lse[0:16], jnp.zeros((112, 128), F32)], axis=0).T
    MA[...] = jnp.exp2(ma * C2 - lse_t) * (1.0 / HM)
    MB[...] = jnp.exp2(mb * C2 - lse_t) * (1.0 / HM)

    def target(slot):
        for part, ref in ((0, MA), (1, MB)):
            w = jnp.sum(jnp.where(lane == slot, ref[...], 0.0), axis=1, keepdims=True)
            row = jnp.sum(E[part, slot] * w, axis=0, keepdims=True)
            for t in range(4):
                T[part * 4 + t, pl.ds(slot, 1), :] = row[:, t * 256:(t + 1) * 256]

    loop(0, 16, target)
    li = lse[16:32]
    li = jnp.concatenate([li, li], axis=1)
    loss = jnp.zeros((16, 1), F32)
    for t in range(8):
        shifted = LM[t] - li
        tt = T[t]
        loss = loss - jnp.sum(tt * shifted, axis=1, keepdims=True) * LN2
        T[t] = jnp.exp2(shifted) - tt

    lane16 = lax.broadcasted_iota(jnp.int32, (16, 128), 1)
    WGP[...] = jnp.where(lane16 == 64, loss, 0.0)

    def back(i):
        for h in range(2):
            zz = zm(z + 4 - 2 * i - h)
            rows = pl.ds(pl.multiple_of(zz * 128, 128), 128)
            hb = HB[pl.ds(zz * 8, 8)]
            hb = jnp.concatenate([hb, hb], axis=2)
            acc = jnp.zeros((8, 16, 128), F32)
            for t in range(8):
                aff = AFF[t, rows, :].reshape(8, 16, 256)
                delta = T[t][None]
                sg = jnp.where(aff > 0.0, delta * hb, 0.0)
                SG[t, h * 128:(h + 1) * 128, :] = sg.reshape(128, 256).astype(BF)
                prod = delta * jnp.maximum(aff, 0.0)
                acc = acc + prod[:, :, 0:128] + prod[:, :, 128:256]
            got = jnp.sum(acc, axis=2, keepdims=True) * ISCALE
            wg = WGP[...]
            for n in range(8):
                cs, ys = n // 4, n % 4
                j = (ys // 2) * 32 + zz * 4 + (ys % 2) * 2 + cs
                wg = jnp.where(lane16 == j, got[n], wg)
            WGP[...] = wg
        total = jnp.zeros((256, 128), F32)
        for t in range(8):
            kt = (ik if t < 4 else IK2)[(t % 4) * 256:(t % 4 + 1) * 256, :]
            total = total + dot(SG[t], kt)
        for h in range(2):
            zz = zm(z + 4 - 2 * i - h)
            RSB[pl.ds(zz * 2, 2)] = total[h * 128:(h + 1) * 128].reshape(2, 4, 16, 128)
            for cs in range(2):
                gg = zz * 2 + cs

                @pl.when(gg != g)
                def _():
                    rs_copy(gg, g).start()

    loop(0, 4, back)
    others(16, g, lambda gg: wg_copy(gg, g).start())
    WGR[g] = WGP[...]
    RSR[g] = RSB[g]
    others(16, g, lambda gg: rs_copy(gg, gg).wait_recv())
    qg = RSR[0]
    for gg in range(1, 16):
        qg = qg + RSR[gg]
    DISP[...] = qg.astype(BF)
    others(16, by, lambda n: dq_copy(n, by).start())
    QGA[by] = DISP[y]
    others(16, g, lambda gg: wg_copy(gg, gg).wait_recv())
    wg = WGR[0]
    for gg in range(1, 16):
        wg = wg + WGR[gg]
    WGS[...] = wg
    others(16, by, lambda n: dw_copy(n, by).start())
    WGA[by] = WGS[...]

    others(4, b, lambda bb: [lx_copy(bb, t, bb).wait_recv() for t in range(2)])
    others(16, by, lambda n: dq_copy(n, n).wait_recv())
    for t in range(2):
        o = jnp.zeros((192, 128), F32)
        for bb in range(4):
            o = o + dot(LTX[bb, t], QGA[bb * 4:(bb + 1) * 4].reshape(64, 128))
        OUTP[t] = o.reshape(4, 48, 128)
        for uu in range(4):

            @pl.when(not_self(t, uu))
            def _():
                o_copy(t, uu, u).start()

    @pl.when(b == 0)
    def _():
        out_q[:, pl.ds(pl.multiple_of(c * 128, 128), 128)] = OUTP[0, u]

    others(4, b, lambda bb: hx_copy(bb, bb).wait_recv())
    others(16, by, lambda n: dw_copy(n, n).wait_recv())
    gw = jnp.zeros((224, 128), F32)
    for bb in range(4):
        gw = gw + dot(HTX[bb], WGA[bb * 4:(bb + 1) * 4].reshape(64, 128).astype(BF))
    out_w[...] = jnp.where(yh == 0, gw[:, 0:32], gw[:, 32:64])
    out_l[...] = WGA[pl.ds(b * 4, 4)].reshape(64, 128)

    for t in range(2):
        for uu in range(4):

            @pl.when(not_self(t, uu))
            def _():
                cols = pl.ds(pl.multiple_of((zm(z + b + 4 * t) * 4 + uu) * 128, 128), 128)
                remote(
                    OUTP.at[t, uu], out_q.at[:, cols], s_o.at[t * 4 + uu], r_o.at[t * 4 + uu],
                    a_dev(zm(z + b + 4 * t), uu),
                ).wait_recv()

        others(4, b, lambda bb: ox_copy(bb, t, b).start())
    for t in range(2):

        def arrive(bb):
            cols = pl.ds(pl.multiple_of(zm(z + bb + 4 * t) * 512, 512), 512)
            remote(
                out_q.at[:, cols], out_q.at[:, cols],
                s_ox.at[bb * 2 + t], r_ox.at[bb * 2 + t], x_dev(bb),
            ).wait_recv()

        others(4, b, arrive)

    mp_copy.wait_send()
    for one in ik_copies + mk_copies:
        one.wait_send()
    for kind, n in (("ra", 4), ("la", 3), ("rb", 3), ("lb", 4)):
        for k in range(n):
            ring(kind, k).wait_send()

    def twins(zz):
        to_twin(zz, "a").wait_send()
        to_twin(zz, "b").wait_send()

    loop(0, 8, twins)

    def a_sends(i):
        t, uu = i // 4, i % 4

        @pl.when(not_self(t, uu))
        def _():
            w_copy(t, uu, u).wait_send()
            o_copy(t, uu, u).wait_send()

    loop(0, 8, a_sends)

    def x_sends(bb):
        wx_copy(bb, b).wait_send()
        hx_copy(bb, b).wait_send()
        for t in range(2):
            lx_copy(bb, t, b).wait_send()
            ox_copy(bb, t, b).wait_send()

    others(4, b, x_sends)

    def y_sends(yy):
        iqy_copy(yy, y).wait_send()
        hwy_copy(yy, y).wait_send()

    others(4, y, y_sends)

    def g_sends(gg):
        iqg_copy(gg, g).wait_send()
        hwg_copy(gg, g).wait_send()
        st_copy(gg, g).wait_send()
        rs_copy(gg, g).wait_send()
        wg_copy(gg, g).wait_send()

    others(16, g, g_sends)

    def by_sends(n):
        dq_copy(n, by).wait_send()
        dw_copy(n, by).wait_send()

    others(16, by, by_sends)


def per_device(
    q_latent, hidden, main_queries, main_keys, index_keys, positions, w_query, w_weights
):
    c = lax.axis_index("ctx")
    yh = lax.axis_index("head")
    y = yh * 2 + (c // 2) % 2
    rows_hidden = w_weights.shape[0]

    def by_group(x):
        x = x.reshape(8, 2, 2, 2, -1).transpose(3, 1, 0, 2, 4)
        return x.reshape(64, -1)

    latent = by_group(q_latent[0])
    lat8 = latent.reshape(64, 8, 192).transpose(1, 0, 2)
    lat_t = latent.T.reshape(8, 192, 64)
    hid = by_group(lax.dynamic_slice_in_dim(hidden[0], c * rows_hidden, rows_hidden, 1))
    hid_t = hid.T
    pos = lax.dynamic_slice_in_dim(by_group(positions[0][:, None])[:, 0], y * 16, 16, 0)
    pos_v = jnp.broadcast_to(pos[:, None], (16, 128))
    ww = jnp.concatenate([w_weights, jnp.zeros((rows_hidden, 96), BF)], axis=1)
    ww = jnp.where(yh == 0, ww, jnp.roll(ww, 32, axis=1))

    vm = pl.BlockSpec(memory_space=pltpu.VMEM)
    dma = pltpu.SemaphoreType.DMA
    sems = []
    for n in (8, 4, 4, 16, 4, 16, 1, 4, 3, 3, 4, 8, 8, 4, 16, 16, 16, 16, 16, 8, 4, 8, 8):
        sems += [dma((n,)), dma((n,))]
    out_q, out_w, out_l = pl.pallas_call(
        kernel,
        out_shape=(
            jax.ShapeDtypeStruct((48, 4096), F32),
            jax.ShapeDtypeStruct((224, 32), F32),
            jax.ShapeDtypeStruct((64, 128), F32),
        ),
        in_specs=[pl.BlockSpec(memory_space=pltpu.SMEM)] + [vm] * 10,
        out_specs=(vm, vm, vm),
        scratch_shapes=[
            pltpu.VMEM((4, 2, 4, 48, 128), BF),
            pltpu.VMEM((4, 16, 128), BF),
            pltpu.VMEM((4, 16, 128), BF),
            pltpu.VMEM((16, 4, 16, 128), BF),
            pltpu.VMEM((4, 16, 128), F32),
            pltpu.VMEM((4, 16, 128), F32),
            pltpu.VMEM((16, 128), F32),
            pltpu.VMEM((16, 16, 128), F32),
            pltpu.VMEM((64, 16, 128), F32),
            pltpu.VMEM((16, 2, 64, DL), BF),
            pltpu.VMEM((1024, DL), BF),
            pltpu.VMEM((1024, DI), BF),
            pltpu.VMEM((2, 16, 128, 1024), F32),
            pltpu.VMEM((128, 128), F32),
            pltpu.VMEM((128, 128), F32),
            pltpu.VMEM((128, 128), F32),
            pltpu.VMEM((128, 128), F32),
            pltpu.VMEM((32, 128), F32),
            pltpu.VMEM((16, 32, 128), F32),
            pltpu.VMEM((8, 1024, 256), F32),
            pltpu.VMEM((8, 16, 256), F32),
            pltpu.VMEM((8, 16, 256), F32),
            pltpu.VMEM((8, 256, 256), BF),
            pltpu.VMEM((16, 4, 16, 128), F32),
            pltpu.VMEM((16, 4, 16, 128), F32),
            pltpu.VMEM((16, 128), F32),
            pltpu.VMEM((16, 16, 128), F32),
            pltpu.VMEM((4, 16, 128), BF),
            pltpu.VMEM((16, 16, 128), BF),
            pltpu.VMEM((16, 128), F32),
            pltpu.VMEM((16, 16, 128), F32),
            pltpu.VMEM((4, 2, 192, 64), BF),
            pltpu.VMEM((4, 224, 64), BF),
            pltpu.VMEM((2, 4, 48, 128), F32),
        ]
        + sems,
        compiler_params=pltpu.CompilerParams(
            collective_id=0, has_side_effects=True, vmem_limit_bytes=56 * 1024 * 1024
        ),
        name="indexer_step",
    )(pos, pos_v, lat8, lat_t, hid, hid_t, main_queries[0], main_keys[0], index_keys[0], w_query, ww)
    loss = out_l[:, 64].reshape(2, 2, 8, 2).transpose(2, 1, 3, 0).reshape(1, 64)
    return out_q, out_w, loss


def solution(mesh):
    return jax.shard_map(
        per_device,
        mesh=mesh,
        in_specs=(
            P("dp", None, None),
            P("dp", None, None),
            P("dp", "ctx", "head", None),
            P("dp", "ctx", None),
            P("dp", "ctx", None),
            P("dp", None),
            P("ctx", "head"),
            P("ctx", "head"),
        ),
        out_specs=(P("ctx", "head"), P("ctx", "head"), P("dp", None)),
        check_vma=False,
    )
```

time: 573 us -> 129 us (0.23)
  blocking collectives: 348 us -> 0 us
  Pallas kernels: 0 us -> 111 us
  waiting for transfers between devices: 110 us -> 0 us
  matrix products: 63.1 us -> 0 us
  other arithmetic: 19.4 us -> 2.05 us
  between operations: 14.7 us -> 0.77 us
    psum x2 -> x0, blocking collectives: 131 us -> none  [the longest x1 117 us: per_device(): lax.psum((query_grad, weight_grad, loss_part), 'ctx')]
    all_gather x3 -> x0, blocking collectives: 114 us -> none  [the longest x2 73.2 us: merged(): everything = jax.tree.map(lambda part: lax.all_gather(part, axis), x)]
    pallas_call x0 -> x1, Pallas kernels: none -> 111 us  [per_device(): pl.pallas_call(kernel, out_shape=(jax.ShapeDtypeStruct((48, 4096), F32),...]
    unnamed x1 -> x0, blocking collectives: 103 us -> none
    psum x2 -> x0, waiting for transfers between devices: 76.5 us -> none  [the longest x1 41.2 us: per_device(): logits = lax.psum(partial_logits, 'head')]
    dot_general x22 -> x0, matrix products: 63.1 us -> none  [the longest x16 48.7 us: block_scores(): jnp.einsum('qhd,sd->qhs', block, key_main, preferred_element_type=jnp.flo...]
    all_gather x2 -> x0, waiting for transfers between devices: 32.6 us -> none  [the longest x1 32.6 us: per_device(): gathered = lax.all_gather(main_queries[0], 'ctx', axis=0, tiled=True)]
    reduce_sum x11 -> x0, other arithmetic: 13.3 us -> none  [the longest x8 6.29 us: local_moments(): return (local_max, jnp.sum(shifted, axis=2))]
  transfers between devices with their start and end apart: 4 -> 0, of which waited for: 3 -> 0; matrix products, arithmetic and copies ran while one was open for 12% -> 0% of each run, Pallas kernels for 0% -> 0%
where the time goes in v1:
time: 129 us; the launch traced here: 127 us
  Pallas kernels  111 us (86%)
  local copies, waits for them, and re-layouts  13.7 us (11%)
  other arithmetic  2.05 us (2%)
    pallas_call x1, Pallas kernels, per_device(): pl.pallas_call(kernel, out_shape=(jax.ShapeDtypeStruct((48, 4096), F32),...  111 us
    unnamed x13, local copies, waits for them, and re-layouts  6.47 us

profile of v1, /device:TPU:1, one launch (start us, length us, event | category | flops | bytes accessed | tf_op | source)
XLA Modules:
  0.0 127.4 jit_solution(5335774927766761495)
XLA Ops:
  0.6 0.0 copy-start
  0.7 0.5 broadcast.12
  1.2 1.3 %reduce.5 = s32[64]{0:T(128)S(1)} reduce(s32[1,64]{1,0:T(1,128)} %param.13, s32[]{:T(128)} %broadcast.12), dimensions={0}, to_apply=%param.13.reduce_sub_computation.3 | reduce | bytes 516 | tf_op args[5]
  2.5 0.1 reshape_broadcast_in_dim_squeeze.3
  2.6 0.2 copy.18
  2.8 0.1 squeeze_reshape.3
  3.0 0.1 dynamic_slice.6.pos_s
  3.0 0.0 copy-start.3
  3.0 0.7 broadcast_in_dim.2.pos_v
  3.7 0.0 copy-done
  3.7 0.1 constant_dynamic-slice_fusion
  3.9 0.0 copy-start.2
  3.9 0.8 copy.25
  4.8 0.7 pad_select_fusion.ww
  5.5 0.7 copy.23
  6.2 1.1 reshape_squeeze.6
  7.3 0.2 copy.31
  7.5 0.1 reshape.24
  7.6 0.3 reshape_reshape.3
  7.8 0.8 copy.30
  8.6 0.0 copy-done.3
  8.6 0.0 copy-done.2
  8.6 0.9 copy.21
  9.5 0.0 copy-done.1
  9.5 1.4 %copy.24 = bf16[1,1024,576]{2,1,0:T(8,128)(2,1)} copy(bf16[1,1024,576]{1,2,0:T(8,128)(2,1)S(1)} %copy-done.1) | data formatting | bytes 2359296 | tf_op args[3]
  11.0 110.9 %indexer_step.1 = (f32[48,4096]{1,0:T(8,128)}, f32[224,32]{1,0:T(8,128)}, f32[64,128]{1,0:T(8,128)}) custom-call(s32[16]{0:T(128)} %copy-done.3, s32[16,128]{1,0:T(8,128)} %broadcast_in_dim.2.pos_v, bf16[8,64,192]{2,1,0:T(8,128)(2,1)} %bitcast.23, bf16[8,192,64]{2,1,0:T(8,128)(2,1)} %bitcast.22, bf16[64,224]{1,0:T(8,128)(2,1)} %copy-done.2, ...), custom_call_target="tpu_custom_call" | custom-call | tf_op jit(solution)/shard_map/indexer_step/pallas_call | solution.py:578
  121.9 0.9 slice_reduce_fusion
  122.8 0.1 reshape_squeeze.7
  122.9 0.2 copy.26
  123.1 0.6 reshape.28
  123.8 1.6 %copy.27 = f32[224,32]{0,1:T(8,128)} copy(f32[224,32]{1,0:T(8,128)} %get-tuple-element.13) | data formatting | bytes 57344
  125.4 2.1 %copy.33 = f32[48,4096]{1,0:T(8,128)} copy(f32[48,4096]{1,0:T(8,128)} %get-tuple-element.18) | data formatting | bytes 1572864
  (5 shorter events, 0.1 us)
Async XLA Ops:
  0.6 3.1 %copy-start = (bf16[1,64,7168]{2,1,0:T(8,128)(2,1)S(1)}, bf16[1,64,7168]{2,1,0:T(8,128)(2,1)}, u32[]{:S(2)}) copy-start(bf16[1,64,7168]{2,1,0:T(8,128)(2,1)} %param.9) | copy-start | bytes 2752516
  3.0 5.6 %copy-start.3 = (s32[16]{0:T(128)}, s32[16]{0:T(128)S(1)}, u32[]{:S(2)}) copy-start(s32[16]{0:T(128)S(1)} %dynamic_slice.6.pos_s) | copy-start | bytes 196
  3.9 4.7 %copy-start.2 = (bf16[64,224]{1,0:T(8,128)(2,1)}, bf16[64,224]{1,0:T(8,128)(2,1)S(1)}, u32[]{:S(2)}) copy-start(bf16[64,224]{1,0:T(8,128)(2,1)S(1)} %reshape.27.hid) | copy-start | bytes 86020
  6.2 3.3 %copy-start.1 = (bf16[1,1024,576]{1,2,0:T(8,128)(2,1)S(1)}, bf16[1,1024,576]{1,2,0:T(8,128)(2,1)}, u32[]{:S(2)}) copy-start(bf16[1,1024,576]{1,2,0:T(8,128)(2,1)} %param.11) | copy-start | bytes 3538948

commit v2 on v1

v2 whole, which is shorter than its diff:
```python
import jax
import jax.numpy as jnp
from jax import lax
from jax.experimental import pallas as pl
from jax.experimental.pallas import tpu as pltpu
from jax.sharding import PartitionSpec as P

HI = 64
DI = 128
HM = 128
DL = 576
MESH = pl.DeviceIdType.MESH
BF = jnp.bfloat16
F32 = jnp.float32

LOG2E = 1.4426950408889634
LN2 = 0.6931471805599453
C2 = 192.0 ** (-0.5) * LOG2E
ISCALE = (HI * DI) ** (-0.5)
FLOOR = -1e30
LOW = -1e29

NT = (((1,), (1,)), ((), ()))
NN = (((1,), (0,)), ((), ()))
TN = (((0,), (0,)), ((), ()))


def dot(a, b, dims=NN):
    return lax.dot_general(a, b, dims, preferred_element_type=F32)


def log2(x):
    return jnp.log(x) * LOG2E


def remote(src, dst, ss, rs, dev):
    return pltpu.make_async_remote_copy(
        src_ref=src, dst_ref=dst, send_sem=ss, recv_sem=rs, device_id=dev, device_id_type=MESH
    )


def loop(lo, hi, body):
    def turn(i, carry):
        body(i)
        return carry

    lax.fori_loop(lo, hi, turn, 0)


def kernel(
    pos_s, lat_h, hid_h, mq_h, mk_h, ik_h, wq_h, ww_h,
    out_q, out_w, out_l,
    LATN, HIDW, MQL, K1, IK1, WQ, WWT, WWF, LAT8, HID, LTF, HTX, WB, PJ, IQP, IQY, IQG,
    HWL, HWY, HWS, HWG, HB, MQ, K2, IK2, E, MA, LA, MS, ST, STG, SI, SIG, AFF, LM, T, SG,
    RSB, RSR, WGP, WGR, DISP, QGA, WGS, WGA, OUTP, GWT,
    s_in,
    s_w, r_w, s_pj, r_pj, s_iqg, r_iqg, s_hwy, r_hwy, s_hwg, r_hwg,
    s_mp, r_mp, s_ra, r_ra, s_la, r_la, s_rb, r_rb, s_lb, r_lb, s_ca, r_ca, s_cb, r_cb,
    s_ik, r_ik, s_k, r_k, s_st, r_st, s_si, r_si, s_rs, r_rs, s_wg, r_wg, s_dq, r_dq, s_dw, r_dw,
    s_lx, r_lx, s_hx, r_hx, s_o, r_o, s_ox, r_ox,
):
    b = lax.axis_index("dp")
    yh = lax.axis_index("head")
    c = lax.axis_index("ctx")
    z = c // 4
    yl = (c // 2) % 2
    core = c % 2
    y = yh * 2 + yl
    u = yl * 2 + core
    g = z * 2 + core
    by = b * 4 + y
    hid_rows = ww_h.shape[1]

    hid_tile = jnp.minimum((c * hid_rows) // 128, 53)
    hid_rest = c * hid_rows - hid_tile * 128
    loads = [
        pltpu.make_async_copy(lat_h, LATN, s_in.at[0]),
        pltpu.make_async_copy(
            hid_h.at[:, pl.ds(pl.multiple_of(hid_tile * 128, 128), 384)], HIDW, s_in.at[1]
        ),
        pltpu.make_async_copy(ww_h, WWT, s_in.at[2]),
        pltpu.make_async_copy(wq_h, WQ, s_in.at[3]),
        pltpu.make_async_copy(mq_h, MQL, s_in.at[4]),
        pltpu.make_async_copy(mk_h, K1, s_in.at[5]),
        pltpu.make_async_copy(ik_h, IK1, s_in.at[6]),
    ]
    for one in loads:
        one.start()

    def g_dev(gg):
        return {"dp": b, "head": yh, "ctx": (gg // 2) * 4 + yl * 2 + gg % 2}

    def y_dev(yy):
        return {"dp": b, "head": yy // 2, "ctx": z * 4 + (yy % 2) * 2 + core}

    def x_dev(bb):
        return {"dp": bb, "head": yh, "ctx": c}

    def by_dev(n):
        yy = n % 4
        return {"dp": n // 4, "head": yy // 2, "ctx": z * 4 + (yy % 2) * 2 + core}

    def a_dev(zz, uu):
        return {"dp": b, "head": yh, "ctx": zz * 4 + uu}

    def zm(v):
        return lax.rem(v + 16, 8)

    def others(n, me, start):
        loop(1, n, lambda d: start(lax.rem(me + d, n)))

    bar = pltpu.get_barrier_semaphore()

    def hello(dev):
        pl.semaphore_signal(bar, inc=1, device_id=dev, device_id_type=MESH)

    others(16, g, lambda gg: hello(g_dev(gg)))
    others(16, by, lambda n: hello(by_dev(n)))

    def not_self(t, uu):
        return jnp.logical_or(b > 0, jnp.logical_or(t > 0, uu != u))

    def hello_a(i):
        t, uu = i // 4, i % 4

        @pl.when(not_self(t, uu))
        def _():
            hello(a_dev(zm(z - b - 4 * t), uu))
            hello(a_dev(zm(z + b + 4 * t), uu))

    loop(0, 8, hello_a)

    row64 = lax.broadcasted_iota(jnp.int32, (64, 64), 0)
    col64 = lax.broadcasted_iota(jnp.int32, (64, 64), 1)

    def natural(r):
        return ((r >> 1) & 7) * 8 + ((r >> 4) & 1) * 4 + (r & 1) * 2 + (r >> 5)

    perm = jnp.where(natural(row64) == col64, 1.0, 0.0).astype(BF)
    WWF[...] = jnp.zeros_like(WWF)
    loads[0].wait()
    lat = dot(perm, LATN[...]).astype(BF)
    for p in range(8):
        LAT8[p] = lat[:, p * 192:(p + 1) * 192]
    loads[1].wait()
    loads[2].wait()
    WWF[pl.ds(pl.multiple_of(yh * 32, 32), 32), :] = WWT[...]
    sel_row = lax.broadcasted_iota(jnp.int32, (384, hid_rows), 0)
    sel_col = lax.broadcasted_iota(jnp.int32, (384, hid_rows), 1)
    sel = jnp.where(sel_row == sel_col + hid_rest, 1.0, 0.0).astype(BF)
    HID[...] = dot(perm, dot(HIDW[...], sel).astype(BF)).astype(BF)
    HWL[...] = dot(HID[...], WWF[...], NT).reshape(4, 16, 128)
    for one in loads[3:]:
        one.wait()
    pl.semaphore_wait(bar, jnp.where(b == 0, 44, 46))

    def w_copy(t, uu, slot):
        zd = zm(z - b - 4 * t)
        cols = pl.ds(pl.multiple_of((zd * 4 + uu) * 128, 128), 128)
        return remote(
            WQ.at[:, cols], WB.at[t, u], s_w.at[t * 4 + uu], r_w.at[t * 4 + slot], a_dev(zd, uu)
        )

    def pj_copy(n, slot):
        return remote(PJ.at[n], IQP.at[slot], s_pj.at[n], r_pj.at[slot], by_dev(n))

    def iqg_copy(gg, slot):
        return remote(IQY, IQG.at[slot], s_iqg.at[gg], r_iqg.at[slot], g_dev(gg))

    def hwy_copy(yy, slot):
        return remote(HWL.at[yy], HWY.at[slot], s_hwy.at[yy], r_hwy.at[slot], y_dev(yy))

    def hwg_copy(gg, slot):
        return remote(HWS, HWG.at[slot], s_hwg.at[gg], r_hwg.at[slot], g_dev(gg))

    def st_copy(gg, slot):
        return remote(ST, STG.at[slot], s_st.at[gg], r_st.at[slot], g_dev(gg))

    def si_copy(gg, slot):
        return remote(SI, SIG.at[slot], s_si.at[gg], r_si.at[slot], g_dev(gg))

    def rs_copy(gg, slot):
        return remote(RSB.at[gg], RSR.at[slot], s_rs.at[gg], r_rs.at[slot], g_dev(gg))

    def wg_copy(gg, slot):
        return remote(WGP, WGR.at[slot], s_wg.at[gg], r_wg.at[slot], g_dev(gg))

    def dq_copy(n, slot):
        return remote(DISP.at[n % 4], QGA.at[slot], s_dq.at[n], r_dq.at[slot], by_dev(n))

    def dw_copy(n, slot):
        return remote(WGS, WGA.at[slot], s_dw.at[n], r_dw.at[slot], by_dev(n))

    def lx_copy(bb, t, slot):
        return remote(
            LAT8.at[zm(z + bb + 4 * t)], LTF.at[t, slot],
            s_lx.at[bb * 2 + t], r_lx.at[slot * 2 + t], x_dev(bb),
        )

    def hx_copy(bb, slot):
        return remote(HID, HTX.at[slot], s_hx.at[bb], r_hx.at[slot], x_dev(bb))

    def out_cols(zz, uu, n):
        return pl.ds(pl.multiple_of((zz * 4 + uu) * 128, 128), n * 128)

    def o_copy(t, uu):
        return remote(
            OUTP.at[t, uu], out_q.at[:, out_cols(z, u, 1)], s_o.at[t * 4 + uu], r_o.at[t * 4 + u],
            a_dev(zm(z + b + 4 * t), uu),
        )

    def o_arrival(t, uu):
        zz = zm(z - b - 4 * t)
        return remote(
            OUTP.at[t, uu], out_q.at[:, out_cols(zz, uu, 1)], s_o.at[t * 4 + uu],
            r_o.at[t * 4 + uu], a_dev(zz, uu),
        )

    def ox_copy(bb, t):
        cols = out_cols(zm(z - b - 4 * t), 0, 4)
        return remote(
            out_q.at[:, cols], out_q.at[:, cols], s_ox.at[bb * 2 + t], r_ox.at[b * 2 + t], x_dev(bb)
        )

    def ox_arrival(bb, t):
        cols = out_cols(zm(z - bb - 4 * t), 0, 4)
        return remote(
            out_q.at[:, cols], out_q.at[:, cols], s_ox.at[bb * 2 + t], r_ox.at[bb * 2 + t], x_dev(bb)
        )

    right = {"dp": b, "head": yh, "ctx": zm(z + 1) * 4 + u}
    left = {"dp": b, "head": yh, "ctx": zm(z - 1) * 4 + u}
    twin = {"dp": b, "head": yh, "ctx": z * 4 + yl * 2 + (1 - core)}

    def piece(zz, half):
        return MQ.at[zz * 2 + core, half]

    def ring(kind, k):
        half = yh if kind[1] == "a" else 1 - yh
        zz = zm(z - k) if kind[0] == "r" else zm(z + k)
        ss, rs = {"ra": (s_ra, r_ra), "la": (s_la, r_la), "rb": (s_rb, r_rb), "lb": (s_lb, r_lb)}[kind]
        return remote(
            piece(zz, half), piece(zz, half), ss.at[k], rs.at[k], right if kind[0] == "r" else left
        )

    def to_twin(zz, which):
        half = yh if which == "a" else 1 - yh
        ss, rs = (s_ca, r_ca) if which == "a" else (s_cb, r_cb)
        return remote(piece(zz, half), piece(zz, half), ss.at[zz], rs.at[zz], twin)

    partner = {"dp": b, "head": 1 - yh, "ctx": c}
    mp_copy = remote(MQL.at[1 - yh], MQ.at[g, yh], s_mp.at[0], r_mp.at[0], partner)
    up = y_dev(lax.rem(y + 1, 4))
    down = y_dev(lax.rem(y + 3, 4))

    def ik_copy(h):
        return remote(
            IK1.at[h * 4:(h + 1) * 4], IK2.at[:, h], s_ik.at[h], r_ik.at[h], down if h else up
        )

    def k_copy(h, i):
        return remote(
            K1.at[:, pl.ds(pl.multiple_of(h * 512 + i * 128, 128), 128)],
            K2.at[i, :, h * 128:(h + 1) * 128],
            s_k.at[h * 4 + i], r_k.at[h * 4 + i], down if h else up,
        )

    def w_start(i):
        t, uu = i // 4, i % 4

        @pl.when(not_self(t, uu))
        def _():
            w_copy(t, uu, u).start()

    loop(0, 8, w_start)
    mp_copy.start()
    others(4, b, lambda bb: [lx_copy(bb, t, b).start() for t in range(2)])
    MQ[g, yh] = MQL[yh]
    ring("ra", 0).start()
    ring("la", 0).start()
    to_twin(z, "a").start()
    others(4, y, lambda yy: hwy_copy(yy, y).start())

    def k_start(i):
        k_copy(0, i).start()
        k_copy(1, i).start()

    loop(0, 4, k_start)
    for h in range(2):
        ik_copy(h).start()
    HWY[y] = HWL[y]

    @pl.when(b == 0)
    def _():
        WB[0, u] = WQ[:, pl.ds(pl.multiple_of(c * 128, 128), 128)]

    for t in range(2):
        LTF[t, b] = LAT8[zm(z + b + 4 * t)]
    HTX[b] = HID[...]
    MA[...] = jnp.zeros_like(MA)
    LA[...] = jnp.zeros_like(LA)

    mp_copy.wait_recv()
    ring("rb", 0).start()
    ring("lb", 0).start()
    to_twin(z, "b").start()

    lane = lax.broadcasted_iota(jnp.int32, (128, 128), 1)
    near_row = lax.broadcasted_iota(jnp.int32, (1, 1024), 1) + c * 1024
    col256 = lax.broadcasted_iota(jnp.int32, (1, 256), 1)
    far_row = (z * 4 + (1 - yl) * 2 + core) * 1024 + (col256 >> 7) * 512 + (col256 & 127)

    def position(slot):
        return pos_s[0, (slot // 2) * 8 + (slot % 2) * 2 + 4 * yl + yh]

    def scores(zz, keys, key_row, part, cols):
        q = MQ[pl.ds(zz * 2, 2)].reshape(256, DL)
        s = dot(q, keys)
        for i in range(2):
            slot = zz * 2 + i
            vis = key_row <= position(slot)
            si = jnp.where(vis, s[i * 128:(i + 1) * 128], FLOOR)
            m = jnp.maximum(jnp.max(si, axis=1, keepdims=True), LOW)
            e = jnp.exp2((si - m) * C2)
            E[slot, :, cols] = e
            here = lane == part * 16 + slot
            MA[...] = jnp.where(here, m, MA[...])
            LA[...] = jnp.where(here, jnp.sum(e, axis=1, keepdims=True), LA[...])

    def near(zz):
        to_twin(zz, "a").wait_recv()
        to_twin(zz, "b").wait_recv()
        scores(zz, K1[...], near_row, 0, pl.ds(0, 1024))

    def step(k):
        ring("ra", k).wait_recv()
        if k < 3:
            ring("ra", k + 1).start()
        to_twin(zm(z - 1 - k), "a").start()
        if k < 3:
            ring("la", k).wait_recv()
            if k < 2:
                ring("la", k + 1).start()
            to_twin(zm(z + 1 + k), "a").start()
            ring("rb", k).wait_recv()
            if k < 2:
                ring("rb", k + 1).start()
            to_twin(zm(z - 1 - k), "b").start()
        ring("lb", k).wait_recv()
        if k < 3:
            ring("lb", k + 1).start()
        to_twin(zm(z + 1 + k), "b").start()

    step(0)
    near(z)

    def w_wait(i):
        t, uu = i // 4, i % 4

        @pl.when(not_self(t, uu))
        def _():
            w_copy(t, uu, uu).wait_recv()

    loop(0, 8, w_wait)
    others(4, b, lambda bb: [lx_copy(bb, t, bb).wait_recv() for t in range(2)])
    PJ[...] = (
        dot(LTF[0].reshape(256, 192), WB[0].reshape(192, 128))
        + dot(LTF[1].reshape(256, 192), WB[1].reshape(192, 128))
    ).reshape(16, 16, 128)
    others(16, by, lambda n: pj_copy(n, by).start())
    IQP[by] = PJ[by]
    others(4, y, lambda yy: hwy_copy(yy, yy).wait_recv())
    HWS[...] = HWY[0] + HWY[1] + HWY[2] + HWY[3]
    others(16, g, lambda gg: hwg_copy(gg, g).start())
    HWG[g] = HWS[...]
    others(4, b, lambda bb: hx_copy(bb, b).start())
    step(1)
    others(16, by, lambda n: pj_copy(n, n).wait_recv())
    for ys in range(4):
        IQY[ys] = (IQP[ys] + IQP[4 + ys] + IQP[8 + ys] + IQP[12 + ys]).astype(BF)
    others(16, g, lambda gg: iqg_copy(gg, g).start())
    IQG[g] = IQY[...]
    loop(0, 2, lambda i: near(zm(z - 1 + 2 * i)))
    step(2)
    loop(0, 2, lambda i: near(zm(z - 2 + 4 * i)))
    step(3)
    loop(0, 2, lambda i: near(zm(z - 3 + 6 * i)))
    near(zm(z + 4))

    def far(i):
        k_copy(0, i).wait_recv()
        k_copy(1, i).wait_recv()
        cols = pl.ds(pl.multiple_of(1024 + i * 256, 256), 256)
        loop(0, 8, lambda zz: scores(zz, K2[i], far_row + i * 128, 1 + i, cols))

    loop(0, 4, far)
    MS[...] = MA[...].T
    sums = LA[...].T
    tops = [MS[16 * p:16 * (p + 1)] for p in range(5)]
    mx = tops[0]
    for p in range(1, 5):
        mx = jnp.maximum(mx, tops[p])
    total = jnp.zeros((16, 128), F32)
    for p in range(5):
        total = total + sums[16 * p:16 * (p + 1)] * jnp.exp2((tops[p] - mx) * C2)
    ST[...] = mx * C2 + log2(jnp.maximum(total, 1e-37))
    others(16, g, lambda gg: st_copy(gg, g).start())
    STG[g] = ST[...]

    others(16, g, lambda gg: hwg_copy(gg, gg).wait_recv())
    hw = HWG[0]
    for gg in range(1, 16):
        hw = hw + HWG[gg]
    hw = hw * ISCALE
    for gg in range(16):
        for ys in range(4):
            j = (ys // 2) * 32 + (gg // 2) * 4 + (ys % 2) * 2 + gg % 2
            HB[gg * 4 + ys] = jnp.broadcast_to(hw[:, j:j + 1], (16, 128))
    sub256 = lax.broadcasted_iota(jnp.int32, (16, 256), 0)
    posq = jnp.zeros((16, 256), jnp.int32)
    for slot in range(16):
        posq = jnp.where(sub256 == slot, position(slot), posq)
    others(16, g, lambda gg: iqg_copy(gg, gg).wait_recv())
    for h in range(2):
        ik_copy(h).wait_recv()

    def index_tile(kt, tile, key_row):
        aff = dot(IQG[...].reshape(1024, 128), kt.reshape(256, 128), NT)
        AFF[tile] = aff
        total = jnp.zeros((16, 256), F32)
        for p in range(64):
            hb = HB[p]
            total = total + jnp.maximum(aff[p * 16:(p + 1) * 16], 0.0) * jnp.concatenate([hb, hb], axis=1)
        LM[tile] = jnp.where(key_row <= posq, total * LOG2E, FLOOR)

    loop(0, 4, lambda i: index_tile(IK1[pl.ds(i * 2, 2)], i, col256 + (c * 1024 + i * 256)))
    loop(0, 4, lambda i: index_tile(IK2[i], i + 4, far_row + i * 128))
    lm = LM[...]
    im = jnp.maximum(jnp.max(jnp.max(lm, axis=0), axis=1, keepdims=True), LOW)
    il = jnp.sum(jnp.sum(jnp.exp2(lm - im[None]), axis=0), axis=1, keepdims=True)
    lane16 = lax.broadcasted_iota(jnp.int32, (16, 128), 1)
    diag = lane16 == lax.broadcasted_iota(jnp.int32, (16, 128), 0)
    il = im + log2(jnp.maximum(il, 1e-37))
    SI[...] = jnp.broadcast_to(jnp.sum(jnp.where(diag, il, 0.0), axis=0, keepdims=True), (8, 128))
    others(16, g, lambda gg: si_copy(gg, g).start())
    SIG[g] = SI[...]

    others(16, g, lambda gg: st_copy(gg, gg).wait_recv())
    stats = STG[...]
    top = jnp.max(stats, axis=0)
    lse = top + log2(jnp.sum(jnp.exp2(stats - top[None]), axis=0))
    weights = [jnp.exp2(MS[16 * p:16 * (p + 1)] * C2 - lse) * (1.0 / HM) for p in range(5)]
    MA[...] = jnp.concatenate(weights + [jnp.zeros((48, 128), F32)], axis=0).T

    def target(slot):
        for p in range(5):
            w = jnp.sum(jnp.where(lane == p * 16 + slot, MA[...], 0.0), axis=1, keepdims=True)
            lo, hi = (0, 1024) if p == 0 else (768 + 256 * p, 1024 + 256 * p)
            row = jnp.sum(E[slot, :, lo:hi] * w, axis=0, keepdims=True)
            for t in range(lo // 256, hi // 256):
                T[t, pl.ds(slot, 1), :] = row[:, t * 256 - lo:t * 256 - lo + 256]

    loop(0, 16, target)
    others(16, g, lambda gg: si_copy(gg, gg).wait_recv())
    istats = SIG[...]
    itop = jnp.max(istats, axis=0)
    li = (itop + log2(jnp.sum(jnp.exp2(istats - itop[None]), axis=0)))[0:1]
    li = jnp.sum(jnp.where(diag, li, 0.0), axis=1, keepdims=True)
    loss = jnp.zeros((16, 1), F32)
    for t in range(8):
        shifted = LM[t] - li
        tt = T[t]
        loss = loss - jnp.sum(tt * shifted, axis=1, keepdims=True) * LN2
        T[t] = jnp.exp2(shifted) - tt

    WGP[...] = jnp.where(lane16 == 64, loss, 0.0)

    def back(i):
        for h in range(2):
            zz = zm(z + 4 - 2 * i - h)
            rows = pl.ds(pl.multiple_of(zz * 128, 128), 128)
            hb = HB[pl.ds(zz * 8, 8)]
            hb = jnp.concatenate([hb, hb], axis=2)
            acc = jnp.zeros((8, 16, 128), F32)
            for t in range(8):
                aff = AFF[t, rows, :].reshape(8, 16, 256)
                delta = T[t][None]
                sg = jnp.where(aff > 0.0, delta * hb, 0.0)
                SG[t, h * 128:(h + 1) * 128, :] = sg.reshape(128, 256).astype(BF)
                prod = delta * jnp.maximum(aff, 0.0)
                acc = acc + prod[:, :, 0:128] + prod[:, :, 128:256]
            got = jnp.sum(acc, axis=2, keepdims=True) * ISCALE
            wg = WGP[...]
            for n in range(8):
                cs, ys = n // 4, n % 4
                j = (ys // 2) * 32 + zz * 4 + (ys % 2) * 2 + cs
                wg = jnp.where(lane16 == j, got[n], wg)
            WGP[...] = wg
        total = jnp.zeros((256, 128), F32)
        for t in range(8):
            kt = IK1[2 * t:2 * t + 2] if t < 4 else IK2[t - 4]
            total = total + dot(SG[t], kt.reshape(256, 128))
        for h in range(2):
            zz = zm(z + 4 - 2 * i - h)
            part = total[h * 128:(h + 1) * 128].reshape(2, 4, 16, 128)
            RSB[pl.ds(zz * 2, 2)] = part.astype(BF)
            for cs in range(2):
                gg = zz * 2 + cs

                @pl.when(gg != g)
                def _():
                    rs_copy(gg, g).start()

    loop(0, 4, back)
    others(16, g, lambda gg: wg_copy(gg, g).start())
    WGR[g] = WGP[...]
    RSR[g] = RSB[g]

    mp_copy.wait_send()
    for h in range(2):
        ik_copy(h).wait_send()

    def k_sent(i):
        k_copy(0, i).wait_send()
        k_copy(1, i).wait_send()

    loop(0, 4, k_sent)
    for kind, n in (("ra", 4), ("la", 3), ("rb", 3), ("lb", 4)):
        for k in range(n):
            ring(kind, k).wait_send()

    def twins(zz):
        to_twin(zz, "a").wait_send()
        to_twin(zz, "b").wait_send()

    loop(0, 8, twins)

    def w_sent(i):
        t, uu = i // 4, i % 4

        @pl.when(not_self(t, uu))
        def _():
            w_copy(t, uu, u).wait_send()

    loop(0, 8, w_sent)

    def x_sent(bb):
        hx_copy(bb, b).wait_send()
        for t in range(2):
            lx_copy(bb, t, b).wait_send()

    others(4, b, x_sent)
    others(4, y, lambda yy: hwy_copy(yy, y).wait_send())

    def g_sent(gg):
        iqg_copy(gg, g).wait_send()
        hwg_copy(gg, g).wait_send()
        st_copy(gg, g).wait_send()
        si_copy(gg, g).wait_send()

    others(16, g, g_sent)
    others(16, by, lambda n: pj_copy(n, by).wait_send())

    others(16, g, lambda gg: rs_copy(gg, gg).wait_recv())
    qg = RSR[0].astype(F32)
    for gg in range(1, 16):
        qg = qg + RSR[gg].astype(F32)
    DISP[...] = qg.astype(BF)
    others(16, by, lambda n: dq_copy(n, by).start())
    QGA[by] = DISP[y]
    others(16, g, lambda gg: wg_copy(gg, gg).wait_recv())
    wg = WGR[0]
    for gg in range(1, 16):
        wg = wg + WGR[gg]
    WGS[...] = wg
    others(16, by, lambda n: dw_copy(n, by).start())
    WGA[by] = WGS[...]

    others(16, by, lambda n: dq_copy(n, n).wait_recv())
    for t in range(2):
        OUTP[t] = dot(LTF[t].reshape(256, 192), QGA[...].reshape(256, 128), TN).reshape(4, 48, 128)
        for uu in range(4):

            @pl.when(not_self(t, uu))
            def _():
                o_copy(t, uu).start()

    @pl.when(b == 0)
    def _():
        out_q[:, out_cols(z, u, 1)] = OUTP[0, u]

    others(4, b, lambda bb: hx_copy(bb, bb).wait_recv())
    others(16, by, lambda n: dw_copy(n, n).wait_recv())
    wg_all = WGA[...].reshape(256, 128)
    GWT[...] = dot(wg_all.astype(BF), HTX[...].reshape(256, hid_rows), TN)
    out_w[...] = GWT[pl.ds(pl.multiple_of(yh * 32, 32), 32), :]
    own = WGA[pl.ds(b * 4, 4)].reshape(64, 128)
    row = lax.broadcasted_iota(jnp.int32, (64, 128), 0)
    col = lax.broadcasted_iota(jnp.int32, (64, 128), 1)
    losses = jnp.where(natural(row) == col, own[:, 64:65], 0.0)
    out_l[...] = jnp.sum(losses, axis=0, keepdims=True)[:, 0:64]

    for t in range(2):
        for uu in range(4):

            @pl.when(not_self(t, uu))
            def _():
                o_arrival(t, uu).wait_recv()

        others(4, b, lambda bb: ox_copy(bb, t).start())

    def g_left(gg):
        rs_copy(gg, g).wait_send()
        wg_copy(gg, g).wait_send()

    others(16, g, g_left)

    def by_left(n):
        dq_copy(n, by).wait_send()
        dw_copy(n, by).wait_send()

    others(16, by, by_left)
    for t in range(2):
        for uu in range(4):

            @pl.when(not_self(t, uu))
            def _():
                o_copy(t, uu).wait_send()

    for t in range(2):
        others(4, b, lambda bb: ox_arrival(bb, t).wait_recv())
    for t in range(2):
        others(4, b, lambda bb: ox_copy(bb, t).wait_send())


def per_device(
    q_latent, hidden, main_queries, main_keys, index_keys, positions, w_query, w_weights
):
    hid_rows = w_weights.shape[0]
    vm = pl.BlockSpec(memory_space=pltpu.VMEM)
    hbm = pl.BlockSpec(memory_space=pl.ANY)
    dma = pltpu.SemaphoreType.DMA
    sems = [dma((7,))]
    for n in (8, 16, 16, 4, 16, 1, 4, 3, 3, 4, 8, 8, 2, 8, 16, 16, 16, 16, 16, 16, 8, 4, 8, 8):
        sems += [dma((n,)), dma((n,))]
    out_q, out_w, out_l = pl.pallas_call(
        kernel,
        out_shape=(
            jax.ShapeDtypeStruct((48, 4096), F32),
            jax.ShapeDtypeStruct((32, hid_rows), F32),
            jax.ShapeDtypeStruct((1, 64), F32),
        ),
        in_specs=[pl.BlockSpec(memory_space=pltpu.SMEM)] + [hbm] * 7,
        out_specs=(vm, vm, vm),
        scratch_shapes=[
            pltpu.VMEM((64, 1536), BF),
            pltpu.VMEM((64, 384), BF),
            pltpu.VMEM((2, 64, DL), BF),
            pltpu.VMEM((DL, 1024), BF),
            pltpu.VMEM((8, 128, DI), BF),
            pltpu.VMEM((48, 4096), BF),
            pltpu.VMEM((32, hid_rows), BF),
            pltpu.VMEM((128, hid_rows), BF),
            pltpu.VMEM((8, 64, 192), BF),
            pltpu.VMEM((64, hid_rows), BF),
            pltpu.VMEM((2, 4, 64, 192), BF),
            pltpu.VMEM((4, 64, hid_rows), BF),
            pltpu.VMEM((2, 4, 48, 128), BF),
            pltpu.VMEM((16, 16, 128), F32),
            pltpu.VMEM((16, 16, 128), F32),
            pltpu.VMEM((4, 16, 128), BF),
            pltpu.VMEM((16, 4, 16, 128), BF),
            pltpu.VMEM((4, 16, 128), F32),
            pltpu.VMEM((4, 16, 128), F32),
            pltpu.VMEM((16, 128), F32),
            pltpu.VMEM((16, 16, 128), F32),
            pltpu.VMEM((64, 16, 128), F32),
            pltpu.VMEM((16, 2, 64, DL), BF),
            pltpu.VMEM((4, DL, 256), BF),
            pltpu.VMEM((4, 2, 128, DI), BF),
            pltpu.VMEM((16, 128, 2048), F32),
            pltpu.VMEM((128, 128), F32),
            pltpu.VMEM((128, 128), F32),
            pltpu.VMEM((128, 128), F32),
            pltpu.VMEM((16, 128), F32),
            pltpu.VMEM((16, 16, 128), F32),
            pltpu.VMEM((8, 128), F32),
            pltpu.VMEM((16, 8, 128), F32),
            pltpu.VMEM((8, 1024, 256), F32),
            pltpu.VMEM((8, 16, 256), F32),
            pltpu.VMEM((8, 16, 256), F32),
            pltpu.VMEM((8, 256, 256), BF),
            pltpu.VMEM((16, 4, 16, 128), BF),
            pltpu.VMEM((16, 4, 16, 128), BF),
            pltpu.VMEM((16, 128), F32),
            pltpu.VMEM((16, 16, 128), F32),
            pltpu.VMEM((4, 16, 128), BF),
            pltpu.VMEM((16, 16, 128), BF),
            pltpu.VMEM((16, 128), F32),
            pltpu.VMEM((16, 16, 128), F32),
            pltpu.VMEM((2, 4, 48, 128), F32),
            pltpu.VMEM((128, hid_rows), F32),
        ]
        + sems,
        compiler_params=pltpu.CompilerParams(
            collective_id=0, has_side_effects=True, vmem_limit_bytes=56 * 1024 * 1024
        ),
        name="indexer_step",
    )(
        positions, q_latent[0], hidden[0], main_queries[0], main_keys[0].T,
        index_keys[0].reshape(8, 128, DI), w_query, w_weights.T,
    )
    return out_q, out_w.T, out_l


def solution(mesh):
    return jax.shard_map(
        per_device,
        mesh=mesh,
        in_specs=(
            P("dp", None, None),
            P("dp", None, None),
            P("dp", "ctx", "head", None),
            P("dp", "ctx", None),
            P("dp", "ctx", None),
            P("dp", None),
            P("ctx", "head"),
            P("ctx", "head"),
        ),
        out_specs=(P("ctx", "head"), P("ctx", "head"), P("dp", None)),
        check_vma=False,
    )
```

time: 129 us -> 111 us (0.86)
  local copies, waits for them, and re-layouts: 13.7 us -> 3.2 us
  Pallas kernels: 111 us -> 106 us
  other arithmetic: 2.05 us -> 0 us
    pallas_call x1, Pallas kernels: 111 us -> 106 us  [per_device(): pl.pallas_call(kernel, out_shape=(jax.ShapeDtypeStruct((48, 4096), F32),...]
    unnamed x13 -> x7, local copies, waits for them, and re-layouts: 6.47 us -> 3.2 us
    another operation x7 -> x0, local copies, waits for them, and re-layouts: 2.61 us -> none  [the longest x3 1.37 us: by_group(): x = x.reshape(8, 2, 2, 2, -1).transpose(3, 1, 0, 2, 4)]
    reshape x5 -> x0, local copies, waits for them, and re-layouts: 1.5 us -> none  [the longest x3 0.84 us: by_group(): return x.reshape(64, -1)]
    transpose x4 -> x0, local copies, waits for them, and re-layouts: 1.35 us -> none  [the longest x1 0.92 us: per_device(): lat_t = latent.T.reshape(8, 192, 64)]
    unnamed x1 -> x0, other arithmetic: 1.32 us -> none
where the time goes in v2:
time: 111 us; the launch traced here: 110 us
  Pallas kernels  106 us (95%)
  local copies, waits for them, and re-layouts  3.2 us (3%)
    pallas_call x1, Pallas kernels, per_device(): pl.pallas_call(kernel, out_shape=(jax.ShapeDtypeStruct((48, 4096), F32),...  106 us
    unnamed x7, local copies, waits for them, and re-layouts  3.2 us

profile of v2, /device:TPU:1, one launch (start us, length us, event | category | flops | bytes accessed | tf_op | source)
XLA Modules:
  0.0 110.2 jit_solution(4370700902007957223)
XLA Ops:
  0.6 106.3 %indexer_step.1 = (f32[48,4096]{1,0:T(8,128)}, f32[32,224]{1,0:T(8,128)}, f32[1,64]{1,0:T(1,128)}) custom-call(s32[1,64]{1,0:T(1,128)} %pos_s.1, bf16[64,1536]{1,0:T(8,128)(2,1)} %bitcast.12, bf16[64,7168]{1,0:T(8,128)(2,1)} %bitcast.10, bf16[2,64,576]{2,1,0:T(8,128)(2,1)} %bitcast.13, bf16[576,1024]{1,0:T(8,128)(2,1)} %bitcast.9, ...), custom_call_target="tpu_custom_call" | custom-call | tf_op jit(solution)/shard_map/indexer_step/pallas_call | solution.py:646
  107.0 0.0 copy-start
  107.0 0.0 copy-start.1
  107.0 2.1 %copy.14 = f32[48,4096]{1,0:T(8,128)} copy(f32[48,4096]{1,0:T(8,128)} %get-tuple-element.12) | data formatting | bytes 1572864
  109.1 0.0 copy-done
  109.1 0.6 copy.15
  109.7 0.0 copy-done.1
  109.7 0.5 copy.16
Async XLA Ops:
  107.0 2.1 %copy-start = (f32[32,224]{1,0:T(8,128)S(1)}, f32[32,224]{1,0:T(8,128)}, u32[]{:S(2)}) copy-start(f32[32,224]{1,0:T(8,128)} %get-tuple-element.7) | copy-start | bytes 86020
  107.0 2.7 %copy-start.1 = (f32[1,64]{1,0:T(1,128)S(1)}, f32[1,64]{1,0:T(1,128)}, u32[]{:S(2)}) copy-start(f32[1,64]{1,0:T(1,128)} %get-tuple-element.14) | copy-start | bytes 772

commit v3 on v2

--- a/solution.py
+++ b/solution.py
@@ -51,11 +51,11 @@
     pos_s, lat_h, hid_h, mq_h, mk_h, ik_h, wq_h, ww_h,
     out_q, out_w, out_l,
     LATN, HIDW, MQL, K1, IK1, WQ, WWT, WWF, LAT8, HID, LTF, HTX, WB, PJ, IQP, IQY, IQG,
-    HWL, HWY, HWS, HWG, HB, MQ, K2, IK2, E, MA, LA, MS, ST, STG, SI, SIG, AFF, LM, T, SG,
+    HWL, HWY, HWS, HWG, HWC, HWT, HB, MQ, K2, IK2, E, MA, LA, MS, ST, STG, SI, SIG, AFF, LM, T, SG,
     RSB, RSR, WGP, WGR, DISP, QGA, WGS, WGA, OUTP, GWT,
     s_in,
     s_w, r_w, s_pj, r_pj, s_iqg, r_iqg, s_hwy, r_hwy, s_hwg, r_hwg,
-    s_mp, r_mp, s_ra, r_ra, s_la, r_la, s_rb, r_rb, s_lb, r_lb, s_ca, r_ca, s_cb, r_cb,
+    s_iqt, r_iqt, s_hwt, r_hwt, s_mp, r_mp, s_qa, r_qa, s_qb, r_qb, s_ca, r_ca, s_cb, r_cb,
     s_ik, r_ik, s_k, r_k, s_st, r_st, s_si, r_si, s_rs, r_rs, s_wg, r_wg, s_dq, r_dq, s_dw, r_dw,
     s_lx, r_lx, s_hx, r_hx, s_o, r_o, s_ox, r_ox,
 ):
@@ -164,15 +164,15 @@
     def pj_copy(n, slot):
         return remote(PJ.at[n], IQP.at[slot], s_pj.at[n], r_pj.at[slot], by_dev(n))
 
-    def iqg_copy(gg, slot):
-        return remote(IQY, IQG.at[slot], s_iqg.at[gg], r_iqg.at[slot], g_dev(gg))
+    def iqz_copy(zz, slot):
+        return remote(IQY, IQG.at[core, slot], s_iqg.at[zz], r_iqg.at[slot], a_dev(zz, u))
+
+    def hwz_copy(zz, slot):
+        return remote(HWS, HWG.at[slot], s_hwg.at[zz], r_hwg.at[slot], a_dev(zz, u))
 
     def hwy_copy(yy, slot):
         return remote(HWL.at[yy], HWY.at[slot], s_hwy.at[yy], r_hwy.at[slot], y_dev(yy))
 
-    def hwg_copy(gg, slot):
-        return remote(HWS, HWG.at[slot], s_hwg.at[gg], r_hwg.at[slot], g_dev(gg))
-
     def st_copy(gg, slot):
         return remote(ST, STG.at[slot], s_st.at[gg], r_st.at[slot], g_dev(gg))
 
@@ -228,25 +228,34 @@
             out_q.at[:, cols], out_q.at[:, cols], s_ox.at[bb * 2 + t], r_ox.at[bb * 2 + t], x_dev(bb)
         )
 
-    right = {"dp": b, "head": yh, "ctx": zm(z + 1) * 4 + u}
-    left = {"dp": b, "head": yh, "ctx": zm(z - 1) * 4 + u}
     twin = {"dp": b, "head": yh, "ctx": z * 4 + yl * 2 + (1 - core)}
-
-    def piece(zz, half):
-        return MQ.at[zz * 2 + core, half]
-
-    def ring(kind, k):
-        half = yh if kind[1] == "a" else 1 - yh
-        zz = zm(z - k) if kind[0] == "r" else zm(z + k)
-        ss, rs = {"ra": (s_ra, r_ra), "la": (s_la, r_la), "rb": (s_rb, r_rb), "lb": (s_lb, r_lb)}[kind]
-        return remote(
-            piece(zz, half), piece(zz, half), ss.at[k], rs.at[k], right if kind[0] == "r" else left
-        )
-
-    def to_twin(zz, which):
-        half = yh if which == "a" else 1 - yh
-        ss, rs = (s_ca, r_ca) if which == "a" else (s_cb, r_cb)
-        return remote(piece(zz, half), piece(zz, half), ss.at[zz], rs.at[zz], twin)
+    iqt_copy = remote(IQG.at[core], IQG.at[core], s_iqt.at[0], r_iqt.at[0], twin)
+    hwt_copy = remote(HWC, HWT, s_hwt.at[0], r_hwt.at[0], twin)
+    hops = {
+        "a": ((0, 2), (0, -2), (0, 1), (0, -1), (-2, 1), (2, -1), (-2, 2)),
+        "b": ((0, 2), (0, -2), (0, 1), (0, -1), (-2, 1), (2, -1), (2, -2)),
+    }
+
+    def piece(zz, kind):
+        return MQ.at[zz * 2 + core, yh if kind == "a" else 1 - yh]
+
+    def hop(kind, n):
+        of, far_by = hops[kind][n]
+        ss, rs = (s_qa, r_qa) if kind == "a" else (s_qb, r_qb)
+        zz = zm(z + of)
+        return remote(
+            piece(zz, kind), piece(zz, kind), ss.at[n], rs.at[zz], a_dev(zm(z + far_by), u)
+        )
+
+    def arrival(kind, of):
+        ss, rs = (s_qa, r_qa) if kind == "a" else (s_qb, r_qb)
+        zz = zm(z + of)
+        remote(piece(zz, kind), piece(zz, kind), ss.at[0], rs.at[zz], a_dev(zm(z + of), u)).wait_recv()
+        to_twin(zz, kind).start()
+
+    def to_twin(zz, kind):
+        ss, rs = (s_ca, r_ca) if kind == "a" else (s_cb, r_cb)
+        return remote(piece(zz, kind), piece(zz, kind), ss.at[zz], rs.at[zz], twin)
 
     partner = {"dp": b, "head": 1 - yh, "ctx": c}
     mp_copy = remote(MQL.at[1 - yh], MQ.at[g, yh], s_mp.at[0], r_mp.at[0], partner)
@@ -276,8 +285,8 @@
     mp_copy.start()
     others(4, b, lambda bb: [lx_copy(bb, t, b).start() for t in range(2)])
     MQ[g, yh] = MQL[yh]
-    ring("ra", 0).start()
-    ring("la", 0).start()
+    for n in range(4):
+        hop("a", n).start()
     to_twin(z, "a").start()
     others(4, y, lambda yy: hwy_copy(yy, y).start())
 
@@ -285,9 +294,8 @@
         k_copy(0, i).start()
         k_copy(1, i).start()
 
-    loop(0, 4, k_start)
-    for h in range(2):
-        ik_copy(h).start()
+    k_start(0)
+    k_start(1)
     HWY[y] = HWL[y]
 
     @pl.when(b == 0)
@@ -301,8 +309,8 @@
     LA[...] = jnp.zeros_like(LA)
 
     mp_copy.wait_recv()
-    ring("rb", 0).start()
-    ring("lb", 0).start()
+    for n in range(4):
+        hop("b", n).start()
     to_twin(z, "b").start()
 
     lane = lax.broadcasted_iota(jnp.int32, (128, 128), 1)
@@ -332,28 +340,6 @@
         to_twin(zz, "b").wait_recv()
         scores(zz, K1[...], near_row, 0, pl.ds(0, 1024))
 
-    def step(k):
-        ring("ra", k).wait_recv()
-        if k < 3:
-            ring("ra", k + 1).start()
-        to_twin(zm(z - 1 - k), "a").start()
-        if k < 3:
-            ring("la", k).wait_recv()
-            if k < 2:
-                ring("la", k + 1).start()
-            to_twin(zm(z + 1 + k), "a").start()
-            ring("rb", k).wait_recv()
-            if k < 2:
-                ring("rb", k + 1).start()
-            to_twin(zm(z - 1 - k), "b").start()
-        ring("lb", k).wait_recv()
-        if k < 3:
-            ring("lb", k + 1).start()
-        to_twin(zm(z + 1 + k), "b").start()
-
-    step(0)
-    near(z)
-
     def w_wait(i):
         t, uu = i // 4, i % 4
 
@@ -368,32 +354,75 @@
         + dot(LTF[1].reshape(256, 192), WB[1].reshape(192, 128))
     ).reshape(16, 16, 128)
     others(16, by, lambda n: pj_copy(n, by).start())
+    k_start(2)
+    k_start(3)
+    for h in range(2):
+        ik_copy(h).start()
     IQP[by] = PJ[by]
+
+    for of, n in ((-2, 4), (2, 5)):
+        arrival("a", of)
+        hop("a", n).start()
+        if of == -2:
+            hop("a", 6).start()
+    arrival("a", -1)
+    arrival("a", 1)
     others(4, y, lambda yy: hwy_copy(yy, yy).wait_recv())
     HWS[...] = HWY[0] + HWY[1] + HWY[2] + HWY[3]
-    others(16, g, lambda gg: hwg_copy(gg, g).start())
-    HWG[g] = HWS[...]
+    others(8, z, lambda zz: hwz_copy(zz, z).start())
+    HWG[z] = HWS[...]
     others(4, b, lambda bb: hx_copy(bb, b).start())
-    step(1)
+    near(z)
+    for of, n in ((-2, 4), (2, 5)):
+        arrival("b", of)
+        hop("b", n).start()
+        if of == 2:
+            hop("b", 6).start()
+    arrival("b", -1)
+    arrival("b", 1)
     others(16, by, lambda n: pj_copy(n, n).wait_recv())
     for ys in range(4):
         IQY[ys] = (IQP[ys] + IQP[4 + ys] + IQP[8 + ys] + IQP[12 + ys]).astype(BF)
-    others(16, g, lambda gg: iqg_copy(gg, g).start())
-    IQG[g] = IQY[...]
-    loop(0, 2, lambda i: near(zm(z - 1 + 2 * i)))
-    step(2)
-    loop(0, 2, lambda i: near(zm(z - 2 + 4 * i)))
-    step(3)
-    loop(0, 2, lambda i: near(zm(z - 3 + 6 * i)))
-    near(zm(z + 4))
-
-    def far(i):
+    others(8, z, lambda zz: iqz_copy(zz, z).start())
+    IQG[core, z] = IQY[...]
+
+    def plane(k):
+        return zm(z + jnp.where(lax.rem(k, 2) == 1, (k + 1) // 2, -(k // 2)))
+
+    loop(1, 5, lambda k: near(plane(k)))
+
+    def far(i, lo, hi):
+        cols = pl.ds(pl.multiple_of(1024 + i * 256, 256), 256)
+        loop(lo, hi, lambda k: scores(plane(k), K2[i], far_row + i * 128, 1 + i, cols))
+
+    def k_wait(i):
         k_copy(0, i).wait_recv()
         k_copy(1, i).wait_recv()
-        cols = pl.ds(pl.multiple_of(1024 + i * 256, 256), 256)
-        loop(0, 8, lambda zz: scores(zz, K2[i], far_row + i * 128, 1 + i, cols))
-
-    loop(0, 4, far)
+
+    def far_early(i):
+        k_wait(i)
+        far(i, 0, 5)
+
+    loop(0, 2, far_early)
+    for kind in ("a", "b"):
+        for of in (-3, 3, 4):
+            arrival(kind, of)
+    others(8, z, lambda zz: hwz_copy(zz, zz).wait_recv())
+    hw = HWG[0]
+    for zz in range(1, 8):
+        hw = hw + HWG[zz]
+    HWC[...] = hw
+    hwt_copy.start()
+    others(8, z, lambda zz: iqz_copy(zz, zz).wait_recv())
+    iqt_copy.start()
+    loop(5, 8, lambda k: near(plane(k)))
+    loop(0, 2, lambda i: far(i, 5, 8))
+
+    def far_late(i):
+        k_wait(i)
+        far(i, 0, 8)
+
+    loop(2, 4, far_late)
     MS[...] = MA[...].T
     sums = LA[...].T
     tops = [MS[16 * p:16 * (p + 1)] for p in range(5)]
@@ -407,26 +436,23 @@
     others(16, g, lambda gg: st_copy(gg, g).start())
     STG[g] = ST[...]
 
-    others(16, g, lambda gg: hwg_copy(gg, gg).wait_recv())
-    hw = HWG[0]
-    for gg in range(1, 16):
-        hw = hw + HWG[gg]
-    hw = hw * ISCALE
-    for gg in range(16):
-        for ys in range(4):
-            j = (ys // 2) * 32 + (gg // 2) * 4 + (ys % 2) * 2 + gg % 2
-            HB[gg * 4 + ys] = jnp.broadcast_to(hw[:, j:j + 1], (16, 128))
+    hwt_copy.wait_recv()
+    hw = (HWC[...] + HWT[...]) * ISCALE
+    for p in range(64):
+        cs, zs, ys = p // 32, (p // 4) % 8, p % 4
+        j = (ys // 2) * 32 + zs * 4 + (ys % 2) * 2 + cs
+        HB[p] = jnp.broadcast_to(hw[:, j:j + 1], (16, 128))
     sub256 = lax.broadcasted_iota(jnp.int32, (16, 256), 0)
     posq = jnp.zeros((16, 256), jnp.int32)
     for slot in range(16):
         posq = jnp.where(sub256 == slot, position(slot), posq)
-    others(16, g, lambda gg: iqg_copy(gg, gg).wait_recv())
+    iqt_copy.wait_recv()
     for h in range(2):
         ik_copy(h).wait_recv()
 
     def index_tile(kt, tile, key_row):
         aff = dot(IQG[...].reshape(1024, 128), kt.reshape(256, 128), NT)
-        AFF[tile] = aff
+        AFF[tile] = aff.reshape(2, 512, 256)
         total = jnp.zeros((16, 256), F32)
         for p in range(64):
             hb = HB[p]
@@ -478,17 +504,22 @@
     def back(i):
         for h in range(2):
             zz = zm(z + 4 - 2 * i - h)
-            rows = pl.ds(pl.multiple_of(zz * 128, 128), 128)
-            hb = HB[pl.ds(zz * 8, 8)]
-            hb = jnp.concatenate([hb, hb], axis=2)
-            acc = jnp.zeros((8, 16, 128), F32)
-            for t in range(8):
-                aff = AFF[t, rows, :].reshape(8, 16, 256)
-                delta = T[t][None]
-                sg = jnp.where(aff > 0.0, delta * hb, 0.0)
-                SG[t, h * 128:(h + 1) * 128, :] = sg.reshape(128, 256).astype(BF)
-                prod = delta * jnp.maximum(aff, 0.0)
-                acc = acc + prod[:, :, 0:128] + prod[:, :, 128:256]
+            rows = pl.ds(pl.multiple_of(zz * 64, 64), 64)
+            accs = []
+            for cs in range(2):
+                hb = HB[pl.ds(cs * 32 + zz * 4, 4)]
+                hb = jnp.concatenate([hb, hb], axis=2)
+                acc = jnp.zeros((4, 16, 128), F32)
+                for t in range(8):
+                    aff = AFF[t, cs, rows, :].reshape(4, 16, 256)
+                    delta = T[t][None]
+                    sg = jnp.where(aff > 0.0, delta * hb, 0.0)
+                    top_row = h * 128 + cs * 64
+                    SG[t, top_row:top_row + 64, :] = sg.reshape(64, 256).astype(BF)
+                    prod = delta * jnp.maximum(aff, 0.0)
+                    acc = acc + prod[:, :, 0:128] + prod[:, :, 128:256]
+                accs.append(acc)
+            acc = jnp.concatenate(accs, axis=0)
             got = jnp.sum(acc, axis=2, keepdims=True) * ISCALE
             wg = WGP[...]
             for n in range(8):
@@ -525,9 +556,11 @@
         k_copy(1, i).wait_send()
 
     loop(0, 4, k_sent)
-    for kind, n in (("ra", 4), ("la", 3), ("rb", 3), ("lb", 4)):
-        for k in range(n):
-            ring(kind, k).wait_send()
+    for n in range(7):
+        hop("a", n).wait_send()
+        hop("b", n).wait_send()
+    iqt_copy.wait_send()
+    hwt_copy.wait_send()
 
     def twins(zz):
         to_twin(zz, "a").wait_send()
@@ -553,12 +586,16 @@
     others(4, y, lambda yy: hwy_copy(yy, y).wait_send())
 
     def g_sent(gg):
-        iqg_copy(gg, g).wait_send()
-        hwg_copy(gg, g).wait_send()
         st_copy(gg, g).wait_send()
         si_copy(gg, g).wait_send()
 
     others(16, g, g_sent)
+
+    def z_sent(zz):
+        iqz_copy(zz, z).wait_send()
+        hwz_copy(zz, z).wait_send()
+
+    others(8, z, z_sent)
     others(16, by, lambda n: pj_copy(n, by).wait_send())
 
     others(16, g, lambda gg: rs_copy(gg, gg).wait_recv())
@@ -578,7 +615,8 @@
 
     others(16, by, lambda n: dq_copy(n, n).wait_recv())
     for t in range(2):
-        OUTP[t] = dot(LTF[t].reshape(256, 192), QGA[...].reshape(256, 128), TN).reshape(4, 48, 128)
+        o = dot(LTF[t].reshape(256, 192), QGA[...].reshape(256, 128), TN)
+        OUTP[t] = o.astype(BF).reshape(4, 48, 128)
         for uu in range(4):
 
             @pl.when(not_self(t, uu))
@@ -641,12 +679,12 @@
     hbm = pl.BlockSpec(memory_space=pl.ANY)
     dma = pltpu.SemaphoreType.DMA
     sems = [dma((7,))]
-    for n in (8, 16, 16, 4, 16, 1, 4, 3, 3, 4, 8, 8, 2, 8, 16, 16, 16, 16, 16, 16, 8, 4, 8, 8):
+    for n in (8, 16, 8, 4, 8, 1, 1, 1, 8, 8, 8, 8, 2, 8, 16, 16, 16, 16, 16, 16, 8, 4, 8, 8):
         sems += [dma((n,)), dma((n,))]
     out_q, out_w, out_l = pl.pallas_call(
         kernel,
         out_shape=(
-            jax.ShapeDtypeStruct((48, 4096), F32),
+            jax.ShapeDtypeStruct((48, 4096), BF),
             jax.ShapeDtypeStruct((32, hid_rows), F32),
             jax.ShapeDtypeStruct((1, 64), F32),
         ),
@@ -669,11 +707,13 @@
             pltpu.VMEM((16, 16, 128), F32),
             pltpu.VMEM((16, 16, 128), F32),
             pltpu.VMEM((4, 16, 128), BF),
-            pltpu.VMEM((16, 4, 16, 128), BF),
+            pltpu.VMEM((2, 8, 4, 16, 128), BF),
             pltpu.VMEM((4, 16, 128), F32),
             pltpu.VMEM((4, 16, 128), F32),
             pltpu.VMEM((16, 128), F32),
-            pltpu.VMEM((16, 16, 128), F32),
+            pltpu.VMEM((8, 16, 128), F32),
+            pltpu.VMEM((16, 128), F32),
+            pltpu.VMEM((16, 128), F32),
             pltpu.VMEM((64, 16, 128), F32),
             pltpu.VMEM((16, 2, 64, DL), BF),
             pltpu.VMEM((4, DL, 256), BF),
@@ -686,7 +726,7 @@
             pltpu.VMEM((16, 16, 128), F32),
             pltpu.VMEM((8, 128), F32),
             pltpu.VMEM((16, 8, 128), F32),
-            pltpu.VMEM((8, 1024, 256), F32),
+            pltpu.VMEM((8, 2, 512, 256), F32),
             pltpu.VMEM((8, 16, 256), F32),
             pltpu.VMEM((8, 16, 256), F32),
             pltpu.VMEM((8, 256, 256), BF),
@@ -698,7 +738,7 @@
             pltpu.VMEM((16, 16, 128), BF),
             pltpu.VMEM((16, 128), F32),
             pltpu.VMEM((16, 16, 128), F32),
-            pltpu.VMEM((2, 4, 48, 128), F32),
+            pltpu.VMEM((2, 4, 48, 128), BF),
             pltpu.VMEM((128, hid_rows), F32),
         ]
         + sems,
@@ -710,7 +750,7 @@
         positions, q_latent[0], hidden[0], main_queries[0], main_keys[0].T,
         index_keys[0].reshape(8, 128, DI), w_query, w_weights.T,
     )
-    return out_q, out_w.T, out_l
+    return out_q.astype(F32), out_w.T, out_l
 
 
 def solution(mesh):

time: 111 us -> 96.2 us (0.87)
  Pallas kernels: 106 us -> 92.4 us
  local copies, waits for them, and re-layouts: 3.2 us -> 1.13 us
  other arithmetic: 0 us -> 1.93 us
    pallas_call x1, Pallas kernels: 106 us -> 92.4 us  [per_device(): pl.pallas_call(kernel, out_shape=(jax.ShapeDtypeStruct((48, 4096), BF), j...]
    unnamed x7 -> x6, local copies, waits for them, and re-layouts: 3.2 us -> 1.13 us
    convert_element_type x0 -> x1, other arithmetic: none -> 1.93 us  [per_device(): return (out_q.astype(F32), out_w.T, out_l)]
where the time goes in v3:
time: 96.2 us; the launch traced here: 96.1 us
  Pallas kernels  92.4 us (96%)
  other arithmetic  1.93 us (2%)
  local copies, waits for them, and re-layouts  1.13 us (1%)
    pallas_call x1, Pallas kernels, per_device(): pl.pallas_call(kernel, out_shape=(jax.ShapeDtypeStruct((48, 4096), BF), j...  92.4 us
    convert_element_type x1, other arithmetic, per_device(): return (out_q.astype(F32), out_w.T, out_l)  1.93 us

profile of v3, /device:TPU:1, one launch (start us, length us, event | category | flops | bytes accessed | tf_op | source)
XLA Modules:
  0.0 96.1 jit_solution(16283963295122310324)
XLA Ops:
  0.6 92.4 %indexer_step.1 = (bf16[48,4096]{1,0:T(8,128)(2,1)}, f32[32,224]{1,0:T(8,128)}, f32[1,64]{1,0:T(1,128)}) custom-call(s32[1,64]{1,0:T(1,128)} %pos_s.1, bf16[64,1536]{1,0:T(8,128)(2,1)} %bitcast.12, bf16[64,7168]{1,0:T(8,128)(2,1)} %bitcast.10, bf16[2,64,576]{2,1,0:T(8,128)(2,1)} %bitcast.13, bf16[576,1024]{1,0:T(8,128)(2,1)} %bitcast.9, ...), custom_call_target="tpu_custom_call" | custom-call | tf_op jit(solution)/shard_map/indexer_step/pallas_call | solution.py:684
  93.1 0.0 copy-start
  93.1 0.0 copy-start.1
  93.1 1.9 %convert_element_type.3 = f32[48,4096]{1,0:T(8,128)} convert(bf16[48,4096]{1,0:T(8,128)(2,1)} %get-tuple-element.6) | non-fusion elementwise | flops 196608 | bytes 1179648 | tf_op jit(solution)/shard_map/convert_element_type | solution.py:753
  95.0 0.0 copy-done
  95.0 0.6 copy.13
  95.6 0.0 copy-done.1
  95.6 0.5 copy.14
Async XLA Ops:
  93.1 2.0 %copy-start = (f32[32,224]{1,0:T(8,128)S(1)}, f32[32,224]{1,0:T(8,128)}, u32[]{:S(2)}) copy-start(f32[32,224]{1,0:T(8,128)} %get-tuple-element.7) | copy-start | bytes 86020
  93.1 2.6 %copy-start.1 = (f32[1,64]{1,0:T(1,128)S(1)}, f32[1,64]{1,0:T(1,128)}, u32[]{:S(2)}) copy-start(f32[1,64]{1,0:T(1,128)} %get-tuple-element.14) | copy-start | bytes 772

commit v4 on v3

--- a/solution.py
+++ b/solution.py
@@ -236,29 +236,33 @@
         "b": ((0, 2), (0, -2), (0, 1), (0, -1), (-2, 1), (2, -1), (2, -2)),
     }
 
-    def piece(zz, kind):
-        return MQ.at[zz * 2 + core, yh if kind == "a" else 1 - yh]
+    places = {0: 0, 1: 1, -1: 2, 2: 3, -2: 4, 3: 5, -3: 6, 4: 7, -4: 7}
+
+    def piece(of, kind):
+        return MQ.at[places[of], core, yh if kind == "a" else 1 - yh]
 
     def hop(kind, n):
         of, far_by = hops[kind][n]
         ss, rs = (s_qa, r_qa) if kind == "a" else (s_qb, r_qb)
-        zz = zm(z + of)
-        return remote(
-            piece(zz, kind), piece(zz, kind), ss.at[n], rs.at[zz], a_dev(zm(z + far_by), u)
+        there = of - far_by
+        return remote(
+            piece(of, kind), piece(there, kind), ss.at[n], rs.at[places[there]],
+            a_dev(zm(z + far_by), u),
         )
 
     def arrival(kind, of):
         ss, rs = (s_qa, r_qa) if kind == "a" else (s_qb, r_qb)
-        zz = zm(z + of)
-        remote(piece(zz, kind), piece(zz, kind), ss.at[0], rs.at[zz], a_dev(zm(z + of), u)).wait_recv()
-        to_twin(zz, kind).start()
-
-    def to_twin(zz, kind):
+        here = piece(of, kind)
+        remote(here, here, ss.at[0], rs.at[places[of]], a_dev(zm(z + of), u)).wait_recv()
+        to_twin(places[of], kind).start()
+
+    def to_twin(k, kind):
         ss, rs = (s_ca, r_ca) if kind == "a" else (s_cb, r_cb)
-        return remote(piece(zz, kind), piece(zz, kind), ss.at[zz], rs.at[zz], twin)
+        here = MQ.at[k, core, yh if kind == "a" else 1 - yh]
+        return remote(here, here, ss.at[k], rs.at[k], twin)
 
     partner = {"dp": b, "head": 1 - yh, "ctx": c}
-    mp_copy = remote(MQL.at[1 - yh], MQ.at[g, yh], s_mp.at[0], r_mp.at[0], partner)
+    mp_copy = remote(MQL.at[1 - yh], MQ.at[0, core, yh], s_mp.at[0], r_mp.at[0], partner)
     up = y_dev(lax.rem(y + 1, 4))
     down = y_dev(lax.rem(y + 3, 4))
 
@@ -284,10 +288,10 @@
     loop(0, 8, w_start)
     mp_copy.start()
     others(4, b, lambda bb: [lx_copy(bb, t, b).start() for t in range(2)])
-    MQ[g, yh] = MQL[yh]
+    MQ[0, core, yh] = MQL[yh]
     for n in range(4):
         hop("a", n).start()
-    to_twin(z, "a").start()
+    to_twin(0, "a").start()
     others(4, y, lambda yy: hwy_copy(yy, y).start())
 
     def k_start(i):
@@ -311,7 +315,7 @@
     mp_copy.wait_recv()
     for n in range(4):
         hop("b", n).start()
-    to_twin(z, "b").start()
+    to_twin(0, "b").start()
 
     lane = lax.broadcasted_iota(jnp.int32, (128, 128), 1)
     near_row = lax.broadcasted_iota(jnp.int32, (1, 1024), 1) + c * 1024
@@ -321,24 +325,30 @@
     def position(slot):
         return pos_s[0, (slot // 2) * 8 + (slot % 2) * 2 + 4 * yl + yh]
 
-    def scores(zz, keys, key_row, part, cols):
-        q = MQ[pl.ds(zz * 2, 2)].reshape(256, DL)
+    def plane(k):
+        return zm(z + jnp.where(lax.rem(k, 2) == 1, (k + 1) // 2, -(k // 2)))
+
+    def scores(k, count, keys, key_row, part, cols):
+        q = MQ[pl.ds(k, count)].reshape(count * 256, DL)
         s = dot(q, keys)
-        for i in range(2):
-            slot = zz * 2 + i
+        ma, la = MA[...], LA[...]
+        for i in range(count * 2):
+            slot = plane(k + i // 2) * 2 + i % 2
             vis = key_row <= position(slot)
             si = jnp.where(vis, s[i * 128:(i + 1) * 128], FLOOR)
             m = jnp.maximum(jnp.max(si, axis=1, keepdims=True), LOW)
             e = jnp.exp2((si - m) * C2)
             E[slot, :, cols] = e
             here = lane == part * 16 + slot
-            MA[...] = jnp.where(here, m, MA[...])
-            LA[...] = jnp.where(here, jnp.sum(e, axis=1, keepdims=True), LA[...])
-
-    def near(zz):
-        to_twin(zz, "a").wait_recv()
-        to_twin(zz, "b").wait_recv()
-        scores(zz, K1[...], near_row, 0, pl.ds(0, 1024))
+            ma = jnp.where(here, m, ma)
+            la = jnp.where(here, jnp.sum(e, axis=1, keepdims=True), la)
+        MA[...] = ma
+        LA[...] = la
+
+    def near(k):
+        to_twin(k, "a").wait_recv()
+        to_twin(k, "b").wait_recv()
+        scores(k, 1, K1[...], near_row, 0, pl.ds(0, 1024))
 
     def w_wait(i):
         t, uu = i // 4, i % 4
@@ -372,7 +382,7 @@
     others(8, z, lambda zz: hwz_copy(zz, z).start())
     HWG[z] = HWS[...]
     others(4, b, lambda bb: hx_copy(bb, b).start())
-    near(z)
+    near(0)
     for of, n in ((-2, 4), (2, 5)):
         arrival("b", of)
         hop("b", n).start()
@@ -386,24 +396,18 @@
     others(8, z, lambda zz: iqz_copy(zz, z).start())
     IQG[core, z] = IQY[...]
 
-    def plane(k):
-        return zm(z + jnp.where(lax.rem(k, 2) == 1, (k + 1) // 2, -(k // 2)))
-
-    loop(1, 5, lambda k: near(plane(k)))
-
-    def far(i, lo, hi):
+    loop(1, 5, near)
+
+    def far(i, k, count):
         cols = pl.ds(pl.multiple_of(1024 + i * 256, 256), 256)
-        loop(lo, hi, lambda k: scores(plane(k), K2[i], far_row + i * 128, 1 + i, cols))
-
-    def k_wait(i):
+        scores(k, count, K2[i], far_row + i * 128, 1 + i, cols)
+
+    def far_early(i):
         k_copy(0, i).wait_recv()
         k_copy(1, i).wait_recv()
-
-    def far_early(i):
-        k_wait(i)
         far(i, 0, 5)
 
-    loop(0, 2, far_early)
+    loop(0, 4, far_early)
     for kind in ("a", "b"):
         for of in (-3, 3, 4):
             arrival(kind, of)
@@ -415,14 +419,8 @@
     hwt_copy.start()
     others(8, z, lambda zz: iqz_copy(zz, zz).wait_recv())
     iqt_copy.start()
-    loop(5, 8, lambda k: near(plane(k)))
-    loop(0, 2, lambda i: far(i, 5, 8))
-
-    def far_late(i):
-        k_wait(i)
-        far(i, 0, 8)
-
-    loop(2, 4, far_late)
+    loop(5, 8, near)
+    loop(0, 4, lambda i: far(i, 5, 3))
     MS[...] = MA[...].T
     sums = LA[...].T
     tops = [MS[16 * p:16 * (p + 1)] for p in range(5)]
@@ -715,7 +713,7 @@
             pltpu.VMEM((16, 128), F32),
             pltpu.VMEM((16, 128), F32),
             pltpu.VMEM((64, 16, 128), F32),
-            pltpu.VMEM((16, 2, 64, DL), BF),
+            pltpu.VMEM((8, 2, 2, 64, DL), BF),
             pltpu.VMEM((4, DL, 256), BF),
             pltpu.VMEM((4, 2, 128, DI), BF),
             pltpu.VMEM((16, 128, 2048), F32),

time: 96.2 us -> 89.4 us (0.929)
  Pallas kernels: 92.4 us -> 85.6 us
    pallas_call x1, Pallas kernels: 92.4 us -> 85.6 us  [per_device(): pl.pallas_call(kernel, out_shape=(jax.ShapeDtypeStruct((48, 4096), BF), j...]
where the time goes in v4:
time: 89.4 us; the launch traced here: 89.3 us
  Pallas kernels  85.6 us (96%)
  other arithmetic  1.93 us (2%)
  local copies, waits for them, and re-layouts  1.13 us (1%)
    pallas_call x1, Pallas kernels, per_device(): pl.pallas_call(kernel, out_shape=(jax.ShapeDtypeStruct((48, 4096), BF), j...  85.6 us
    convert_element_type x1, other arithmetic, per_device(): return (out_q.astype(F32), out_w.T, out_l)  1.93 us

profile of v4, /device:TPU:1, one launch (start us, length us, event | category | flops | bytes accessed | tf_op | source)
XLA Modules:
  0.0 89.3 jit_solution(11179475822234192441)
XLA Ops:
  0.6 85.6 %indexer_step.1 = (bf16[48,4096]{1,0:T(8,128)(2,1)}, f32[32,224]{1,0:T(8,128)}, f32[1,64]{1,0:T(1,128)}) custom-call(s32[1,64]{1,0:T(1,128)} %pos_s.1, bf16[64,1536]{1,0:T(8,128)(2,1)} %bitcast.12, bf16[64,7168]{1,0:T(8,128)(2,1)} %bitcast.10, bf16[2,64,576]{2,1,0:T(8,128)(2,1)} %bitcast.13, bf16[576,1024]{1,0:T(8,128)(2,1)} %bitcast.9, ...), custom_call_target="tpu_custom_call" | custom-call | tf_op jit(solution)/shard_map/indexer_step/pallas_call | solution.py:682
  86.2 0.0 copy-start
  86.2 0.0 copy-start.1
  86.2 1.9 %convert_element_type.3 = f32[48,4096]{1,0:T(8,128)} convert(bf16[48,4096]{1,0:T(8,128)(2,1)} %get-tuple-element.6) | non-fusion elementwise | flops 196608 | bytes 1179648 | tf_op jit(solution)/shard_map/convert_element_type | solution.py:751
  88.1 0.0 copy-done
  88.1 0.6 copy.13
  88.8 0.0 copy-done.1
  88.8 0.5 copy.14
Async XLA Ops:
  86.2 2.0 %copy-start = (f32[32,224]{1,0:T(8,128)S(1)}, f32[32,224]{1,0:T(8,128)}, u32[]{:S(2)}) copy-start(f32[32,224]{1,0:T(8,128)} %get-tuple-element.7) | copy-start | bytes 86020
  86.2 2.6 %copy-start.1 = (f32[1,64]{1,0:T(1,128)S(1)}, f32[1,64]{1,0:T(1,128)}, u32[]{:S(2)}) copy-start(f32[1,64]{1,0:T(1,128)} %get-tuple-element.14) | copy-start | bytes 772

commit v5 on v4

--- a/solution.py
+++ b/solution.py
@@ -232,7 +232,7 @@
     iqt_copy = remote(IQG.at[core], IQG.at[core], s_iqt.at[0], r_iqt.at[0], twin)
     hwt_copy = remote(HWC, HWT, s_hwt.at[0], r_hwt.at[0], twin)
     hops = {
-        "a": ((0, 2), (0, -2), (0, 1), (0, -1), (-2, 1), (2, -1), (-2, 2)),
+        "a": ((0, 1), (0, -1), (-1, 1), (1, -1), (-2, 1), (-2, 2), (2, -1)),
         "b": ((0, 2), (0, -2), (0, 1), (0, -1), (-2, 1), (2, -1), (2, -2)),
     }
 
@@ -289,7 +289,7 @@
     mp_copy.start()
     others(4, b, lambda bb: [lx_copy(bb, t, b).start() for t in range(2)])
     MQ[0, core, yh] = MQL[yh]
-    for n in range(4):
+    for n in range(2):
         hop("a", n).start()
     to_twin(0, "a").start()
     others(4, y, lambda yy: hwy_copy(yy, y).start())
@@ -316,6 +316,9 @@
     for n in range(4):
         hop("b", n).start()
     to_twin(0, "b").start()
+    for of, n in ((-1, 2), (1, 3)):
+        arrival("a", of)
+        hop("a", n).start()
 
     lane = lax.broadcasted_iota(jnp.int32, (128, 128), 1)
     near_row = lax.broadcasted_iota(jnp.int32, (1, 1024), 1) + c * 1024
@@ -345,10 +348,11 @@
         MA[...] = ma
         LA[...] = la
 
-    def near(k):
-        to_twin(k, "a").wait_recv()
-        to_twin(k, "b").wait_recv()
-        scores(k, 1, K1[...], near_row, 0, pl.ds(0, 1024))
+    def near(k, count):
+        for i in range(k, k + count):
+            to_twin(i, "a").wait_recv()
+            to_twin(i, "b").wait_recv()
+        scores(k, count, K1[...], near_row, 0, pl.ds(0, 1024))
 
     def w_wait(i):
         t, uu = i // 4, i % 4
@@ -370,19 +374,17 @@
         ik_copy(h).start()
     IQP[by] = PJ[by]
 
-    for of, n in ((-2, 4), (2, 5)):
+    for of, first, last in ((-2, 4, 6), (2, 6, 7)):
         arrival("a", of)
-        hop("a", n).start()
-        if of == -2:
-            hop("a", 6).start()
-    arrival("a", -1)
-    arrival("a", 1)
+        for n in range(first, last):
+            hop("a", n).start()
     others(4, y, lambda yy: hwy_copy(yy, yy).wait_recv())
-    HWS[...] = HWY[0] + HWY[1] + HWY[2] + HWY[3]
+    hw = HWY[0] + HWY[1] + HWY[2] + HWY[3]
+    HWS[...] = jnp.concatenate([hw[0:8, 0:64], hw[8:16, 0:64]], axis=1)
     others(8, z, lambda zz: hwz_copy(zz, z).start())
     HWG[z] = HWS[...]
     others(4, b, lambda bb: hx_copy(bb, b).start())
-    near(0)
+    near(0, 1)
     for of, n in ((-2, 4), (2, 5)):
         arrival("b", of)
         hop("b", n).start()
@@ -396,7 +398,7 @@
     others(8, z, lambda zz: iqz_copy(zz, z).start())
     IQG[core, z] = IQY[...]
 
-    loop(1, 5, near)
+    near(1, 4)
 
     def far(i, k, count):
         cols = pl.ds(pl.multiple_of(1024 + i * 256, 256), 256)
@@ -419,7 +421,7 @@
     hwt_copy.start()
     others(8, z, lambda zz: iqz_copy(zz, zz).wait_recv())
     iqt_copy.start()
-    loop(5, 8, near)
+    near(5, 3)
     loop(0, 4, lambda i: far(i, 5, 3))
     MS[...] = MA[...].T
     sums = LA[...].T
@@ -436,6 +438,7 @@
 
     hwt_copy.wait_recv()
     hw = (HWC[...] + HWT[...]) * ISCALE
+    hw = jnp.concatenate([hw[:, 0:64], hw[:, 64:128]], axis=0)
     for p in range(64):
         cs, zs, ys = p // 32, (p // 4) % 8, p % 4
         j = (ys // 2) * 32 + zs * 4 + (ys % 2) * 2 + cs
@@ -603,6 +606,21 @@
     DISP[...] = qg.astype(BF)
     others(16, by, lambda n: dq_copy(n, by).start())
     QGA[by] = DISP[y]
+
+    others(16, by, lambda n: dq_copy(n, n).wait_recv())
+    for t in range(2):
+        o = dot(LTF[t].reshape(256, 192), QGA[...].reshape(256, 128), TN)
+        OUTP[t] = o.astype(BF).reshape(4, 48, 128)
+        for uu in range(4):
+
+            @pl.when(not_self(t, uu))
+            def _():
+                o_copy(t, uu).start()
+
+    @pl.when(b == 0)
+    def _():
+        out_q[:, out_cols(z, u, 1)] = OUTP[0, u]
+
     others(16, g, lambda gg: wg_copy(gg, gg).wait_recv())
     wg = WGR[0]
     for gg in range(1, 16):
@@ -610,20 +628,14 @@
     WGS[...] = wg
     others(16, by, lambda n: dw_copy(n, by).start())
     WGA[by] = WGS[...]
-
-    others(16, by, lambda n: dq_copy(n, n).wait_recv())
     for t in range(2):
-        o = dot(LTF[t].reshape(256, 192), QGA[...].reshape(256, 128), TN)
-        OUTP[t] = o.astype(BF).reshape(4, 48, 128)
         for uu in range(4):
 
             @pl.when(not_self(t, uu))
             def _():
-                o_copy(t, uu).start()
-
-    @pl.when(b == 0)
-    def _():
-        out_q[:, out_cols(z, u, 1)] = OUTP[0, u]
+                o_arrival(t, uu).wait_recv()
+
+        others(4, b, lambda bb: ox_copy(bb, t).start())
 
     others(4, b, lambda bb: hx_copy(bb, bb).wait_recv())
     others(16, by, lambda n: dw_copy(n, n).wait_recv())
@@ -635,15 +647,6 @@
     col = lax.broadcasted_iota(jnp.int32, (64, 128), 1)
     losses = jnp.where(natural(row) == col, own[:, 64:65], 0.0)
     out_l[...] = jnp.sum(losses, axis=0, keepdims=True)[:, 0:64]
-
-    for t in range(2):
-        for uu in range(4):
-
-            @pl.when(not_self(t, uu))
-            def _():
-                o_arrival(t, uu).wait_recv()
-
-        others(4, b, lambda bb: ox_copy(bb, t).start())
 
     def g_left(gg):
         rs_copy(gg, g).wait_send()
@@ -708,10 +711,10 @@
             pltpu.VMEM((2, 8, 4, 16, 128), BF),
             pltpu.VMEM((4, 16, 128), F32),
             pltpu.VMEM((4, 16, 128), F32),
-            pltpu.VMEM((16, 128), F32),
-            pltpu.VMEM((8, 16, 128), F32),
-            pltpu.VMEM((16, 128), F32),
-            pltpu.VMEM((16, 128), F32),
+            pltpu.VMEM((8, 128), F32),
+            pltpu.VMEM((8, 8, 128), F32),
+            pltpu.VMEM((8, 128), F32),
+            pltpu.VMEM((8, 128), F32),
             pltpu.VMEM((64, 16, 128), F32),
             pltpu.VMEM((8, 2, 2, 64, DL), BF),
             pltpu.VMEM((4, DL, 256), BF),

time: 89.4 us -> 87.7 us (0.981)
  Pallas kernels: 85.6 us -> 83.9 us
    pallas_call x1, Pallas kernels: 85.6 us -> 83.9 us  [per_device(): pl.pallas_call(kernel, out_shape=(jax.ShapeDtypeStruct((48, 4096), BF), j...]
where the time goes in v5:
time: 87.7 us; the launch traced here: 87.6 us
  Pallas kernels  83.9 us (96%)
  other arithmetic  1.93 us (2%)
  local copies, waits for them, and re-layouts  1.13 us (1%)
    pallas_call x1, Pallas kernels, per_device(): pl.pallas_call(kernel, out_shape=(jax.ShapeDtypeStruct((48, 4096), BF), j...  83.9 us
    convert_element_type x1, other arithmetic, per_device(): return (out_q.astype(F32), out_w.T, out_l)  1.93 us

profile of v5, /device:TPU:1, one launch (start us, length us, event | category | flops | bytes accessed | tf_op | source)
XLA Modules:
  0.0 87.6 jit_solution(5182909940151400557)
XLA Ops:
  0.6 83.9 %indexer_step.1 = (bf16[48,4096]{1,0:T(8,128)(2,1)}, f32[32,224]{1,0:T(8,128)}, f32[1,64]{1,0:T(1,128)}) custom-call(s32[1,64]{1,0:T(1,128)} %pos_s.1, bf16[64,1536]{1,0:T(8,128)(2,1)} %bitcast.12, bf16[64,7168]{1,0:T(8,128)(2,1)} %bitcast.10, bf16[2,64,576]{2,1,0:T(8,128)(2,1)} %bitcast.13, bf16[576,1024]{1,0:T(8,128)(2,1)} %bitcast.9, ...), custom_call_target="tpu_custom_call" | custom-call | tf_op jit(solution)/shard_map/indexer_step/pallas_call | solution.py:685
  84.5 0.0 copy-start
  84.5 0.0 copy-start.1
  84.5 1.9 %convert_element_type.3 = f32[48,4096]{1,0:T(8,128)} convert(bf16[48,4096]{1,0:T(8,128)(2,1)} %get-tuple-element.6) | non-fusion elementwise | flops 196608 | bytes 1179648 | tf_op jit(solution)/shard_map/convert_element_type | solution.py:754
  86.5 0.0 copy-done
  86.5 0.6 copy.13
  87.1 0.0 copy-done.1
  87.1 0.5 copy.14
Async XLA Ops:
  84.5 2.0 %copy-start = (f32[32,224]{1,0:T(8,128)S(1)}, f32[32,224]{1,0:T(8,128)}, u32[]{:S(2)}) copy-start(f32[32,224]{1,0:T(8,128)} %get-tuple-element.7) | copy-start | bytes 86020
  84.5 2.6 %copy-start.1 = (f32[1,64]{1,0:T(1,128)S(1)}, f32[1,64]{1,0:T(1,128)}, u32[]{:S(2)}) copy-start(f32[1,64]{1,0:T(1,128)} %get-tuple-element.14) | copy-start | bytes 772

commit v6 on v5

--- a/solution.py
+++ b/solution.py
@@ -50,7 +50,7 @@
 def kernel(
     pos_s, lat_h, hid_h, mq_h, mk_h, ik_h, wq_h, ww_h,
     out_q, out_w, out_l,
-    LATN, HIDW, MQL, K1, IK1, WQ, WWT, WWF, LAT8, HID, LTF, HTX, WB, PJ, IQP, IQY, IQG,
+    LATN, HIDW, MQL, PK, QS, K1, IK1, WQ, WWT, WWF, LAT8, HID, LTF, HTX, WB, PJ, IQP, IQY, IQG,
     HWL, HWY, HWS, HWG, HWC, HWT, HB, MQ, K2, IK2, E, MA, LA, MS, ST, STG, SI, SIG, AFF, LM, T, SG,
     RSB, RSR, WGP, WGR, DISP, QGA, WGS, WGA, OUTP, GWT,
     s_in,
@@ -84,9 +84,6 @@
         pltpu.make_async_copy(mk_h, K1, s_in.at[5]),
         pltpu.make_async_copy(ik_h, IK1, s_in.at[6]),
     ]
-    for one in loads:
-        one.start()
-
     def g_dev(gg):
         return {"dp": b, "head": yh, "ctx": (gg // 2) * 4 + yl * 2 + gg % 2}
 
@@ -107,7 +104,11 @@
         return lax.rem(v + 16, 8)
 
     def others(n, me, start):
-        loop(1, n, lambda d: start(lax.rem(me + d, n)))
+        def turn(i):
+            d = n // 2 + jnp.where(lax.rem(i, 2) == 1, (i + 1) // 2, -(i // 2))
+            start(lax.rem(me + d, n))
+
+        loop(0, n - 1, turn)
 
     bar = pltpu.get_barrier_semaphore()
 
@@ -129,6 +130,8 @@
             hello(a_dev(zm(z + b + 4 * t), uu))
 
     loop(0, 8, hello_a)
+    for one in loads:
+        one.start()
 
     row64 = lax.broadcasted_iota(jnp.int32, (64, 64), 0)
     col64 = lax.broadcasted_iota(jnp.int32, (64, 64), 1)
@@ -152,6 +155,11 @@
     HWL[...] = dot(HID[...], WWF[...], NT).reshape(4, 16, 128)
     for one in loads[3:]:
         one.wait()
+    for n in range(2):
+        x = MQL[n]
+        for p in range(4):
+            PK[n, p * 64:(p + 1) * 64] = x[:, p * 128:(p + 1) * 128]
+        PK[n, 256:288] = jnp.concatenate([x[0:32, 512:576], x[32:64, 512:576]], axis=1)
     pl.semaphore_wait(bar, jnp.where(b == 0, 44, 46))
 
     def w_copy(t, uu, slot):
@@ -232,7 +240,7 @@
     iqt_copy = remote(IQG.at[core], IQG.at[core], s_iqt.at[0], r_iqt.at[0], twin)
     hwt_copy = remote(HWC, HWT, s_hwt.at[0], r_hwt.at[0], twin)
     hops = {
-        "a": ((0, 1), (0, -1), (-1, 1), (1, -1), (-2, 1), (-2, 2), (2, -1)),
+        "a": ((0, 2), (0, -2), (0, 1), (0, -1), (-2, 1), (2, -1), (-3, 1)),
         "b": ((0, 2), (0, -2), (0, 1), (0, -1), (-2, 1), (2, -1), (2, -2)),
     }
 
@@ -262,7 +270,7 @@
         return remote(here, here, ss.at[k], rs.at[k], twin)
 
     partner = {"dp": b, "head": 1 - yh, "ctx": c}
-    mp_copy = remote(MQL.at[1 - yh], MQ.at[0, core, yh], s_mp.at[0], r_mp.at[0], partner)
+    mp_copy = remote(PK.at[1 - yh], MQ.at[0, core, yh], s_mp.at[0], r_mp.at[0], partner)
     up = y_dev(lax.rem(y + 1, 4))
     down = y_dev(lax.rem(y + 3, 4))
 
@@ -288,8 +296,8 @@
     loop(0, 8, w_start)
     mp_copy.start()
     others(4, b, lambda bb: [lx_copy(bb, t, b).start() for t in range(2)])
-    MQ[0, core, yh] = MQL[yh]
-    for n in range(2):
+    MQ[0, core, yh] = PK[yh]
+    for n in range(4):
         hop("a", n).start()
     to_twin(0, "a").start()
     others(4, y, lambda yy: hwy_copy(yy, y).start())
@@ -316,9 +324,6 @@
     for n in range(4):
         hop("b", n).start()
     to_twin(0, "b").start()
-    for of, n in ((-1, 2), (1, 3)):
-        arrival("a", of)
-        hop("a", n).start()
 
     lane = lax.broadcasted_iota(jnp.int32, (128, 128), 1)
     near_row = lax.broadcasted_iota(jnp.int32, (1, 1024), 1) + c * 1024
@@ -332,7 +337,7 @@
         return zm(z + jnp.where(lax.rem(k, 2) == 1, (k + 1) // 2, -(k // 2)))
 
     def scores(k, count, keys, key_row, part, cols):
-        q = MQ[pl.ds(k, count)].reshape(count * 256, DL)
+        q = QS[pl.ds(k, count)].reshape(count * 256, DL)
         s = dot(q, keys)
         ma, la = MA[...], LA[...]
         for i in range(count * 2):
@@ -352,6 +357,13 @@
         for i in range(k, k + count):
             to_twin(i, "a").wait_recv()
             to_twin(i, "b").wait_recv()
+            for n in range(4):
+                x = MQ[i, n // 2, n % 2]
+                rows = slice(n * 64, (n + 1) * 64)
+                for p in range(4):
+                    QS[i, rows, p * 128:(p + 1) * 128] = x[p * 64:(p + 1) * 64]
+                rest = jnp.concatenate([x[256:288, 0:64], x[256:288, 64:128]], axis=0)
+                QS[i, rows, 512:576] = rest
         scores(k, count, K1[...], near_row, 0, pl.ds(0, 1024))
 
     def w_wait(i):
@@ -374,10 +386,11 @@
         ik_copy(h).start()
     IQP[by] = PJ[by]
 
-    for of, first, last in ((-2, 4, 6), (2, 6, 7)):
+    for of, n in ((-2, 4), (2, 5)):
         arrival("a", of)
-        for n in range(first, last):
-            hop("a", n).start()
+        hop("a", n).start()
+    arrival("a", -1)
+    arrival("a", 1)
     others(4, y, lambda yy: hwy_copy(yy, yy).wait_recv())
     hw = HWY[0] + HWY[1] + HWY[2] + HWY[3]
     HWS[...] = jnp.concatenate([hw[0:8, 0:64], hw[8:16, 0:64]], axis=1)
@@ -397,6 +410,8 @@
         IQY[ys] = (IQP[ys] + IQP[4 + ys] + IQP[8 + ys] + IQP[12 + ys]).astype(BF)
     others(8, z, lambda zz: iqz_copy(zz, z).start())
     IQG[core, z] = IQY[...]
+    arrival("a", -3)
+    hop("a", 6).start()
 
     near(1, 4)
 
@@ -410,9 +425,8 @@
         far(i, 0, 5)
 
     loop(0, 4, far_early)
-    for kind in ("a", "b"):
-        for of in (-3, 3, 4):
-            arrival(kind, of)
+    for kind, of in (("a", 3), ("a", 4), ("b", -3), ("b", 3), ("b", 4)):
+        arrival(kind, of)
     others(8, z, lambda zz: hwz_copy(zz, zz).wait_recv())
     hw = HWG[0]
     for zz in range(1, 8):
@@ -672,6 +686,12 @@
         others(4, b, lambda bb: ox_copy(bb, t).wait_send())
 
 
+def widen(q_ref, w_ref, l_ref, out_q, out_w, out_l):
+    out_q[...] = q_ref[...].astype(F32)
+    out_w[...] = w_ref[...]
+    out_l[...] = l_ref[...]
+
+
 def per_device(
     q_latent, hidden, main_queries, main_keys, index_keys, positions, w_query, w_weights
 ):
@@ -695,6 +715,8 @@
             pltpu.VMEM((64, 1536), BF),
             pltpu.VMEM((64, 384), BF),
             pltpu.VMEM((2, 64, DL), BF),
+            pltpu.VMEM((2, 288, 128), BF),
+            pltpu.VMEM((8, 256, DL), BF),
             pltpu.VMEM((DL, 1024), BF),
             pltpu.VMEM((8, 128, DI), BF),
             pltpu.VMEM((48, 4096), BF),
@@ -716,7 +738,7 @@
             pltpu.VMEM((8, 128), F32),
             pltpu.VMEM((8, 128), F32),
             pltpu.VMEM((64, 16, 128), F32),
-            pltpu.VMEM((8, 2, 2, 64, DL), BF),
+            pltpu.VMEM((8, 2, 2, 288, 128), BF),
             pltpu.VMEM((4, DL, 256), BF),
             pltpu.VMEM((4, 2, 128, DI), BF),
             pltpu.VMEM((16, 128, 2048), F32),
@@ -751,7 +773,18 @@
         positions, q_latent[0], hidden[0], main_queries[0], main_keys[0].T,
         index_keys[0].reshape(8, 128, DI), w_query, w_weights.T,
     )
-    return out_q.astype(F32), out_w.T, out_l
+    out_q, out_w, out_l = pl.pallas_call(
+        widen,
+        out_shape=(
+            jax.ShapeDtypeStruct((48, 4096), F32),
+            jax.ShapeDtypeStruct((32, hid_rows), F32),
+            jax.ShapeDtypeStruct((1, 64), F32),
+        ),
+        in_specs=[vm] * 3,
+        out_specs=(vm, vm, vm),
+        name="widen",
+    )(out_q, out_w, out_l)
+    return out_q, out_w.T, out_l
 
 
 def solution(mesh):

time: 87.7 us -> 84.2 us (0.960)
  other arithmetic: 1.93 us -> 0 us
  local copies, waits for them, and re-layouts: 1.13 us -> 0 us
    pallas_call x1, Pallas kernels: 83.9 us -> 81.5 us  [per_device(): pl.pallas_call(kernel, out_shape=(jax.ShapeDtypeStruct((48, 4096), BF), j...]
    pallas_call x0 -> x1, Pallas kernels: none -> 1.96 us  [per_device(): pl.pallas_call(widen, out_shape=(jax.ShapeDtypeStruct((48, 4096), F32), j...]
    convert_element_type x1 -> x0, other arithmetic: 1.93 us -> none  [per_device(): return (out_q.astype(F32), out_w.T, out_l)]
    unnamed x6 -> x0, local copies, waits for them, and re-layouts: 1.13 us -> none
where the time goes in v6:
time: 84.2 us; the launch traced here: 84.1 us
  Pallas kernels  83.4 us (99%)
    pallas_call x1, Pallas kernels, per_device(): pl.pallas_call(kernel, out_shape=(jax.ShapeDtypeStruct((48, 4096), BF), j...  81.5 us
    pallas_call x1, Pallas kernels, per_device(): pl.pallas_call(widen, out_shape=(jax.ShapeDtypeStruct((48, 4096), F32), j...  1.96 us

profile of v6, /device:TPU:1, one launch (start us, length us, event | category | flops | bytes accessed | tf_op | source)
XLA Modules:
  0.0 84.1 jit_solution(6616042824254619172)
XLA Ops:
  0.6 81.5 %indexer_step.1 = (bf16[48,4096]{1,0:T(8,128)(2,1)}, f32[32,224]{1,0:T(8,128)}, f32[1,64]{1,0:T(1,128)}) custom-call(s32[1,64]{1,0:T(1,128)} %pos_s.1, bf16[64,1536]{1,0:T(8,128)(2,1)} %bitcast.12, bf16[64,7168]{1,0:T(8,128)(2,1)} %bitcast.10, bf16[2,64,576]{2,1,0:T(8,128)(2,1)} %bitcast.13, bf16[576,1024]{1,0:T(8,128)(2,1)} %bitcast.9, ...), custom_call_target="tpu_custom_call" | custom-call | tf_op jit(solution)/shard_map/indexer_step/pallas_call | solution.py:705
  82.1 2.0 %widen.1 = (f32[48,4096]{1,0:T(8,128)}, f32[32,224]{1,0:T(8,128)}, f32[1,64]{1,0:T(1,128)}) custom-call(bf16[48,4096]{1,0:T(8,128)(2,1)} %get-tuple-element.9.q_ref, f32[32,224]{1,0:T(8,128)} %get-tuple-element.10.w_ref, f32[1,64]{1,0:T(1,128)} %get-tuple-element.11.l_ref), custom_call_target="tpu_custom_call" | custom-call | tf_op jit(solution)/shard_map/widen/pallas_call | solution.py:776

commit v7 on v6

--- a/solution.py
+++ b/solution.py
@@ -293,8 +293,8 @@
         def _():
             w_copy(t, uu, u).start()
 
+    mp_copy.start()
     loop(0, 8, w_start)
-    mp_copy.start()
     others(4, b, lambda bb: [lx_copy(bb, t, b).start() for t in range(2)])
     MQ[0, core, yh] = PK[yh]
     for n in range(4):
@@ -501,7 +501,7 @@
             for t in range(lo // 256, hi // 256):
                 T[t, pl.ds(slot, 1), :] = row[:, t * 256 - lo:t * 256 - lo + 256]
 
-    loop(0, 16, target)
+    loop(0, 4, lambda i: [target(4 * i + j) for j in range(4)])
     others(16, g, lambda gg: si_copy(gg, gg).wait_recv())
     istats = SIG[...]
     itop = jnp.max(istats, axis=0)

time: 84.2 us -> 83.8 us (level)
  no operation moved by 1% of the time
where the time goes in v7:
time: 83.8 us; the launch traced here: 83.7 us
  Pallas kernels  83.1 us (99%)
    pallas_call x1, Pallas kernels, per_device(): pl.pallas_call(kernel, out_shape=(jax.ShapeDtypeStruct((48, 4096), BF), j...  81.1 us
    pallas_call x1, Pallas kernels, per_device(): pl.pallas_call(widen, out_shape=(jax.ShapeDtypeStruct((48, 4096), F32), j...  1.96 us

profile of v7, /device:TPU:1, one launch (start us, length us, event | category | flops | bytes accessed | tf_op | source)
XLA Modules:
  0.0 83.7 jit_solution(752407268952324419)
XLA Ops:
  0.6 81.1 %indexer_step.1 = (bf16[48,4096]{1,0:T(8,128)(2,1)}, f32[32,224]{1,0:T(8,128)}, f32[1,64]{1,0:T(1,128)}) custom-call(s32[1,64]{1,0:T(1,128)} %pos_s.1, bf16[64,1536]{1,0:T(8,128)(2,1)} %bitcast.12, bf16[64,7168]{1,0:T(8,128)(2,1)} %bitcast.10, bf16[2,64,576]{2,1,0:T(8,128)(2,1)} %bitcast.13, bf16[576,1024]{1,0:T(8,128)(2,1)} %bitcast.9, ...), custom_call_target="tpu_custom_call" | custom-call | tf_op jit(solution)/shard_map/indexer_step/pallas_call | solution.py:705
  81.7 2.0 %widen.1 = (f32[48,4096]{1,0:T(8,128)}, f32[32,224]{1,0:T(8,128)}, f32[1,64]{1,0:T(1,128)}) custom-call(bf16[48,4096]{1,0:T(8,128)(2,1)} %get-tuple-element.9.q_ref, f32[32,224]{1,0:T(8,128)} %get-tuple-element.10.w_ref, f32[1,64]{1,0:T(1,128)} %get-tuple-element.11.l_ref), custom_call_target="tpu_custom_call" | custom-call | tf_op jit(solution)/shard_map/widen/pallas_call | solution.py:776
